TPU v7x, 256 devices: a whole 4x4x8 slice. The times are simulated.
256 devices in a mesh: ctx: 32 (over y, z), fsdp: 8 (over x, core).
Axes of the slice: x: 4, y: 4, z: 8, core: 2. Of those that a mesh axis runs over, the one named last changes fastest.
Arguments:
- tokens: int32 [16384], P('ctx'), may hold values from 0 to 511
- embedding: bfloat16 [512, 4096], P(None, 'fsdp'), may hold values from -6 to 6
- norm_gain: float32 [4096], replicated, may hold values from 0.1 to 1.9
- in_weight: bfloat16 [4096, 3, 2048], P('ctx', None, 'fsdp'), may hold values from -0.09375 to 0.09375
- short_taps: float32 [7, 3, 2048], P(None, None, 'fsdp'), may hold values from -2 to 2
- decay_rates: float32 [16, 128], P(None, 'fsdp'), may hold values from 3.0517578e-05 to 0.1
- residue: float32 [16, 128], P(None, 'fsdp'), may hold values from -0.078125 to 0.078125
- skip_weight: float32 [2048], P('fsdp'), may hold values from -4 to 4
- out_weight: bfloat16 [2048, 4096], P('fsdp', 'ctx'), may hold values from -0.125 to 0.125
Outputs:
- mixed: bfloat16 [16384, 4096], P('ctx', 'fsdp')
All inputs are finite; a program needn't handle non-finite values.
Results may differ from a plain program's by a relative error of at most 0.018.
Values may be sent and summed in bfloat16 or wider, within the bound.
A program may use at most 64 MiB of HBM per device.

v0:
```python
import math

import jax
import jax.numpy as jnp
from jax import lax
from jax.sharding import PartitionSpec as P

GROUP = 16


highest_precision = lax.Precision.HIGHEST


def from_partner(block, axis, apart):
    count = lax.axis_size(axis)
    route = []
    for low in range(count):
        high = low | 1 << apart
        if high != low and high < count:
            route += [(low, high), (high, low)]
    return lax.ppermute(block, axis, route)


def from_behind(value, axis, steps):
    count = lax.axis_size(axis)
    first, last = (max(0, -steps), min(count, count - steps))
    return lax.ppermute(value, axis, [(source, source + steps) for source in range(first, last)])


def direct_dft(real_part, imag_part, direction):
    length = real_part.shape[-1]
    counter = jnp.arange(length, dtype=jnp.int32)
    product = counter[:, None] * counter[None, :] % length
    angles = direction * 2.0 * math.pi / length * product.astype(jnp.float32)
    cosine_table = jnp.cos(angles)
    sine_table = jnp.sin(angles)
    new_real = jnp.dot(real_part, cosine_table, precision=highest_precision) - jnp.dot(
        imag_part, sine_table, precision=highest_precision
    )
    new_imag = jnp.dot(real_part, sine_table, precision=highest_precision) + jnp.dot(
        imag_part, cosine_table, precision=highest_precision
    )
    return (new_real, new_imag)


def transform(real_part, imag_part, direction):
    return direct_dft(real_part, imag_part, direction)


def modal_spectrum(decay_rates, residue, frequency, seq_length):
    rate_grid = decay_rates[:, :, None]
    angle_grid = math.pi / seq_length * frequency
    parity = frequency - 2.0 * jnp.floor(0.5 * frequency)
    tail_term = -jnp.expm1(-rate_grid * seq_length)
    numerator = residue[:, :, None] * (tail_term + parity * (2.0 - 2.0 * tail_term))
    half_sine = jnp.sin(0.5 * angle_grid)
    real_den = 2.0 * half_sine * half_sine + -jnp.expm1(-rate_grid) * jnp.cos(angle_grid)
    imag_den = jnp.exp(-rate_grid) * jnp.sin(angle_grid)
    magnitude = real_den * real_den + imag_den * imag_den
    spec_real = jnp.sum(numerator * real_den / magnitude, axis=0)
    spec_imag = jnp.sum(-numerator * imag_den / magnitude, axis=0)
    return (spec_real, spec_imag)


def section_angle(position, bit_number, tok_count):
    offset = (
        position % (1 << bit_number) * tok_count + jnp.arange(tok_count, dtype=jnp.int32)
    ).astype(jnp.float32)
    angle_grid = -math.pi / ((1 << bit_number) * tok_count) * offset
    is_upper = position // (1 << bit_number) % 2 == 1
    return (jnp.cos(angle_grid), jnp.sin(angle_grid), is_upper)


def forward_section(real_part, imag_part, bit_number, position):
    tok_count = real_part.shape[-1]
    other_real, other_imag = (
        from_partner(real_part.astype(jnp.bfloat16), "ctx", bit_number).astype(real_part.dtype),
        from_partner(imag_part.astype(jnp.bfloat16), "ctx", bit_number).astype(imag_part.dtype),
    )
    cosine, sine_value, is_upper = section_angle(position, bit_number, tok_count)
    diff_real = other_real - real_part
    diff_imag = other_imag - imag_part
    turned_real = diff_real * cosine - diff_imag * sine_value
    turned_imag = diff_real * sine_value + diff_imag * cosine
    new_real = jnp.where(is_upper, turned_real, real_part + other_real)
    new_imag = jnp.where(is_upper, turned_imag, imag_part + other_imag)
    return (new_real, new_imag)


def inverse_section(real_part, imag_part, bit_number, position):
    tok_count = real_part.shape[-1]
    other_real, other_imag = (
        from_partner(real_part.astype(jnp.bfloat16), "ctx", bit_number).astype(real_part.dtype),
        from_partner(imag_part.astype(jnp.bfloat16), "ctx", bit_number).astype(imag_part.dtype),
    )
    cosine, sine_value, is_upper = section_angle(position, bit_number, tok_count)
    rot_other_real = other_real * cosine + other_imag * sine_value
    rot_other_imag = other_imag * cosine - other_real * sine_value
    rot_own_real = real_part * cosine + imag_part * sine_value
    rot_own_imag = imag_part * cosine - real_part * sine_value
    new_real = jnp.where(
        is_upper, 0.5 * (other_real - rot_own_real), 0.5 * (real_part + rot_other_real)
    )
    new_imag = jnp.where(
        is_upper, 0.5 * (other_imag - rot_own_imag), 0.5 * (imag_part + rot_other_imag)
    )
    return (new_real, new_imag)


def by_pairs(pair_real, pair_imag, decay_rates, residue, position):
    tok_count = pair_real.shape[-1]
    ctx_count = lax.axis_size("ctx")
    bit_count = ctx_count.bit_length() - 1
    seq_length = tok_count * ctx_count
    groups_local = decay_rates.shape[1]
    pair_half = GROUP // 2
    times_grid = (position * tok_count + jnp.arange(tok_count, dtype=jnp.int32)).astype(jnp.float32)
    phase_grid = -math.pi / seq_length * times_grid
    cosine = jnp.cos(phase_grid)
    sine_value = jnp.sin(phase_grid)
    odd_real = pair_real * cosine - pair_imag * sine_value
    odd_imag = pair_real * sine_value + pair_imag * cosine
    real_part = jnp.stack([pair_real, odd_real], axis=0)
    imag_part = jnp.stack([pair_imag, odd_imag], axis=0)
    for level in range(bit_count):
        real_part, imag_part = forward_section(
            real_part, imag_part, bit_count - 1 - level, position
        )
    real_part, imag_part = transform(real_part, imag_part, -1.0)
    reversed_index = jnp.zeros((), jnp.int32)
    for level in range(bit_count):
        reversed_index = reversed_index + position // (1 << level) % 2 * (
            1 << bit_count - 1 - level
        )
    local_freq = reversed_index + ctx_count * jnp.arange(tok_count, dtype=jnp.int32)
    frequency = (2 * local_freq[None, :] + jnp.arange(2, dtype=jnp.int32)[:, None]).astype(
        jnp.float32
    )
    spec_real, spec_imag = modal_spectrum(decay_rates, residue, frequency.reshape(-1), seq_length)
    spec_real = jnp.transpose(spec_real.reshape(groups_local, 2, tok_count), (1, 0, 2))[
        :, :, None, :
    ]
    spec_imag = jnp.transpose(spec_imag.reshape(groups_local, 2, tok_count), (1, 0, 2))[
        :, :, None, :
    ]
    grouped_real = real_part.reshape(2, groups_local, pair_half, tok_count)
    grouped_imag = imag_part.reshape(2, groups_local, pair_half, tok_count)
    real_part = (grouped_real * spec_real - grouped_imag * spec_imag).reshape(2, -1, tok_count)
    imag_part = (grouped_real * spec_imag + grouped_imag * spec_real).reshape(2, -1, tok_count)
    real_part, imag_part = transform(real_part, imag_part, 1.0)
    real_part = real_part / tok_count
    imag_part = imag_part / tok_count
    for level in range(bit_count):
        real_part, imag_part = inverse_section(real_part, imag_part, level, position)
    rot_real = real_part[1] * cosine + imag_part[1] * sine_value
    rot_imag = imag_part[1] * cosine - real_part[1] * sine_value
    return (0.5 * (real_part[0] + rot_real), 0.5 * (imag_part[0] + rot_imag))


def body(
    tokens,
    embedding,
    norm_gain,
    in_weight,
    short_taps,
    decay_rates,
    residue,
    skip_weight,
    out_weight,
):
    tok_count = tokens.shape[0]
    vocab_size = embedding.shape[0]
    local_channels = in_weight.shape[2]
    one_hot = (tokens[:, None] == jnp.arange(vocab_size, dtype=jnp.int32)[None, :]).astype(
        jnp.bfloat16
    )
    own_columns = jnp.dot(one_hot, embedding, preferred_element_type=jnp.float32).astype(
        jnp.bfloat16
    )
    features = lax.all_gather(own_columns, "fsdp", axis=1, tiled=True)
    widened = features.astype(jnp.float32)
    mean_square = jnp.mean(widened * widened, axis=1, keepdims=True)
    normed = (widened * lax.rsqrt(mean_square + 1e-05) * norm_gain).astype(jnp.bfloat16)
    block_piece = lax.all_gather(in_weight, "ctx", axis=0, tiled=True)
    panel = block_piece.reshape(block_piece.shape[0], 3 * local_channels)
    projected = jnp.dot(normed, panel, preferred_element_type=jnp.float32)
    projected = projected.reshape(tok_count, 3, local_channels).astype(jnp.bfloat16)
    reach_back = short_taps.shape[0] - 1
    earlier = from_behind(projected[tok_count - reach_back :], "ctx", 1)
    extended = jnp.concatenate([earlier, projected], axis=0).astype(jnp.float32)
    short = jnp.zeros((tok_count, 3, local_channels), jnp.float32)
    for lag_step in range(reach_back + 1):
        short = (
            short
            + short_taps[lag_step]
            * extended[reach_back - lag_step : reach_back - lag_step + tok_count]
        )
    queries = short[:, 0, :]
    driving = short[:, 1, :] * short[:, 2, :]
    groups_local = local_channels // GROUP
    pair_half = GROUP // 2
    flipped = driving.T.reshape(groups_local, 2, pair_half, tok_count)
    pair_real = flipped[:, 0].reshape(groups_local * pair_half, tok_count)
    pair_imag = flipped[:, 1].reshape(groups_local * pair_half, tok_count)
    position = lax.axis_index("ctx")
    conv_real, conv_imag = by_pairs(pair_real, pair_imag, decay_rates, residue, position)
    stacked = jnp.stack(
        [
            conv_real.reshape(groups_local, pair_half, tok_count),
            conv_imag.reshape(groups_local, pair_half, tok_count),
        ],
        axis=1,
    )
    convolved = stacked.reshape(local_channels, tok_count).T
    response = convolved + skip_weight * driving
    gated = (queries * response).astype(jnp.bfloat16)
    partial_out = jnp.dot(
        gated,
        lax.all_gather(out_weight, "ctx", axis=1, tiled=True),
        preferred_element_type=jnp.float32,
    )
    return lax.psum_scatter(
        partial_out.astype(jnp.bfloat16), "fsdp", scatter_dimension=1, tiled=True
    )


def solution(mesh):
    placed = (
        P("ctx"),
        P(None, "fsdp"),
        P(),
        P("ctx", None, "fsdp"),
        P(None, None, "fsdp"),
        P(None, "fsdp"),
        P(None, "fsdp"),
        P("fsdp"),
        P("fsdp", "ctx"),
    )
    return jax.shard_map(
        body, mesh=mesh, in_specs=placed, out_specs=P("ctx", "fsdp"), check_vma=False
    )
```

profile of v0, /device:TPU:16, one launch (start us, length us, event | category | flops | bytes accessed | tf_op | source)
XLA Modules:
  0.0 434.8 jit_solution(17419077178434026112)
XLA Ops:
  7.6 2.0 convolution_convert_fusion.1
  10.6 36.6 %all-gather.4.cloned.1.call-done = bf16[512,4096]{1,0:T(8,128)(2,1)} async-done(((bf16[512,512]{1,0:T(8,128)(2,1)}), bf16[512,4096]{1,0:T(8,128)(2,1)}) %all-gather.4.cloned.1.call-update) | async-done | bytes 4194320 | tf_op jit(solution)/shard_map/all_gather | solution.py:180
  47.1 3.1 fusion
  50.2 92.2 %all-gather.6.cloned.1.call-done = bf16[4096,3,256]{0,2,1:T(8,128)(2,1)} async-done(((bf16[128,3,256]{0,2,1:T(8,128)(2,1)}), bf16[4096,3,256]{0,2,1:T(8,128)(2,1)}) %all-gather.6.cloned.1.call-update) | async-done | bytes 6291472 | tf_op jit(solution)/shard_map/all_gather | solution.py:184
  142.5 7.5 %fusion.15 = bf16[512,3,256]{2,0,1:T(8,128)(2,1)S(1)} fusion(bf16[4096,3,256]{0,2,1:T(8,128)(2,1)} %all-gather.6.cloned.1.call-done, bf16[512,4096]{1,0:T(8,128)(2,1)} %all-gather.4.cloned.1.call-done, f32[4096]{0:T(1024)S(1)} %copy-done.26, f32[512]{0:T(512)S(1)} %add_rsqrt_fusion), kind=kOutput, calls=%fused_computation.29 | convolution fusion | flops 3230007296 | bytes 11290624 | tf_op jit(solution)/shard_map/dot_general | solution.py:186
  150.0 4.1 collective-permute-start
  154.2 3.5 collective-permute-done
  160.3 3.0 collective-permute-start.2
  163.7 4.3 collective-permute-done.1
  167.9 3.0 collective-permute-done.2
  170.9 2.3 fusion.207
  175.3 4.9 %collective-permute-done.3 = bf16[2,128,512]{2,1,0:T(8,128)(2,1)S(1)} collective-permute-done((bf16[2,128,512]{2,1,0:T(8,128)(2,1)}, bf16[2,128,512]{2,1,0:T(8,128)(2,1)S(1)}, u32[]{:S(2)}, u32[]{:S(2)}) %collective-permute-start.3) | collective-permute-done | bytes 262176 | tf_op jit(solution)/shard_map/ppermute | solution.py:21
  180.2 2.8 collective-permute-done.4
  183.7 2.3 fusion.203
  186.0 2.4 collective-permute-start.5
  188.4 3.6 collective-permute-start.6
  192.7 8.9 %collective-permute-done.5 = bf16[2,128,512]{2,1,0:T(8,128)(2,1)S(1)} collective-permute-done((bf16[2,128,512]{2,1,0:T(8,128)(2,1)}, bf16[2,128,512]{2,1,0:T(8,128)(2,1)S(1)}, u32[]{:S(2)}, u32[]{:S(2)}) %collective-permute-start.5) | collective-permute-done | bytes 262176 | tf_op jit(solution)/shard_map/ppermute | solution.py:21
  201.6 4.5 %collective-permute-done.6 = bf16[2,128,512]{2,1,0:T(8,128)(2,1)S(1)} collective-permute-done((bf16[2,128,512]{2,1,0:T(8,128)(2,1)}, bf16[2,128,512]{2,1,0:T(8,128)(2,1)S(1)}, u32[]{:S(2)}, u32[]{:S(2)}) %collective-permute-start.6) | collective-permute-done | bytes 262176 | tf_op jit(solution)/shard_map/ppermute | solution.py:21
  206.1 2.4 fusion.199
  208.5 5.8 %collective-permute-start.7 = (bf16[2,128,512]{2,1,0:T(8,128)(2,1)}, bf16[2,128,512]{2,1,0:T(8,128)(2,1)S(1)}, u32[]{:S(2)}, u32[]{:S(2)}) collective-permute-start(bf16[2,128,512]{2,1,0:T(8,128)(2,1)} %get-tuple-element.27), channel_id=1, source_target_pairs={{0,16},{16,0},{8,24},{24,8},{32,48},{48,32},{40,56},{56,40},{64,80... | collective-permute-start | bytes 786440 | tf_op jit(solution)/shard_map/ppermute | solution.py:21
  214.5 12.7 %collective-permute-done.7 = bf16[2,128,512]{2,1,0:T(8,128)(2,1)S(1)} collective-permute-done((bf16[2,128,512]{2,1,0:T(8,128)(2,1)}, bf16[2,128,512]{2,1,0:T(8,128)(2,1)S(1)}, u32[]{:S(2)}, u32[]{:S(2)}) %collective-permute-start.7) | collective-permute-done | bytes 262176 | tf_op jit(solution)/shard_map/ppermute | solution.py:21
  227.3 2.8 collective-permute-done.8
  230.8 2.3 fusion.195
  238.2 6.1 %collective-permute-done.10 = bf16[2,128,512]{2,1,0:T(8,128)(2,1)S(1)} collective-permute-done((bf16[2,128,512]{2,1,0:T(8,128)(2,1)}, bf16[2,128,512]{2,1,0:T(8,128)(2,1)S(1)}, u32[]{:S(2)}, u32[]{:S(2)}) %collective-permute-start.10) | collective-permute-done | bytes 262176 | tf_op jit(solution)/shard_map/ppermute | solution.py:21
  244.3 5.1 %collective-permute-done.9 = bf16[2,128,512]{2,1,0:T(8,128)(2,1)} collective-permute-done((bf16[2,128,512]{2,1,0:T(8,128)(2,1)}, bf16[2,128,512]{2,1,0:T(8,128)(2,1)}, u32[]{:S(2)}, u32[]{:S(2)}) %collective-permute-start.9) | collective-permute-done | bytes 262176 | tf_op jit(solution)/shard_map/ppermute | solution.py:21
  250.6 5.3 %fusion.33 = f32[2,128,512]{2,1,0:T(8,128)S(1)} fusion(f32[2,128,512]{2,1,0:T(8,128)S(1)} %get-tuple-element.50), kind=kOutput, calls=%fused_computation.48 | convolution fusion | flops 808976384 | bytes 1048576 | tf_op jit(solution)/shard_map/dot_general | solution.py:40
  256.0 5.4 %fusion.31 = f32[2,128,512]{2,1,0:T(8,128)S(1)} fusion(f32[2,128,512]{2,1,0:T(8,128)S(1)} %get-tuple-element.50), kind=kOutput, calls=%fused_computation.46 | convolution fusion | flops 808976384 | bytes 1048576 | tf_op jit(solution)/shard_map/dot_general | solution.py:37
  261.3 5.3 %convolution_add_fusion.1 = f32[2,128,512]{2,1,0:T(8,128)S(1)} fusion(f32[2,128,512]{2,1,0:T(8,128)S(1)} %fusion.33, f32[2,128,512]{2,1,0:T(8,128)S(1)} %get-tuple-element.49), kind=kOutput, calls=%fused_computation.33 | convolution fusion | flops 809107456 | bytes 1572864 | tf_op jit(solution)/shard_map/dot_general | solution.py:40
  266.7 5.5 %convolution_subtract_fusion.1 = f32[2,128,512]{2,1,0:T(8,128)S(1)} fusion(f32[2,128,512]{2,1,0:T(8,128)S(1)} %fusion.31, f32[2,128,512]{2,1,0:T(8,128)S(1)} %get-tuple-element.49), kind=kOutput, calls=%fused_computation.34 | convolution fusion | flops 809107456 | bytes 1572864 | tf_op jit(solution)/shard_map/dot_general | solution.py:37
  272.2 4.9 %fusion.28 = f32[2,128,512]{2,1,0:T(8,128)S(1)} fusion(f32[2,128,512]{2,1,0:T(8,128)S(1)} %convolution_subtract_fusion.1, f32[2,128,512]{2,1,0:T(8,128)S(1)} %convolution_add_fusion.1, f32[2,16,512]{2,1,0:T(8,128)S(1)} %copy.32, f32[2,16,512]{2,1,0:T(8,128)S(1)} %copy-done.5), kind=kOutput, calls=%fused_computation.43 | convolution fusion | flops 809369600 | bytes 1703936 | tf_op jit(solution)/shard_map/dot_general | solution.py:37
  277.1 5.0 %multiply_convert_fusion.1 = (bf16[2,128,512]{2,1,0:T(8,128)(2,1)S(1)}, f32[2,128,512]{2,1,0:T(8,128)S(1)}) fusion(f32[2,128,512]{2,1,0:T(8,128)S(1)} %fusion.28, f32[2,128,512]{2,1,0:T(8,128)S(1)} %convolution_add_fusion.1, f32[2,128,512]{2,1,0:T(8,128)S(1)} %convolution_subtract_fusion.1, f32[2,16,512]{2,1,0:T(8,128)S(1)} %copy.32, ...), kind=kOutput, calls=%fused_computation.200 | convolution fusion | flops 809762816 | bytes 2490368 | tf_op jit(solution)/shard_map/dot_general | solution.py:37
  282.7 5.0 %fusion.24 = f32[2,128,512]{2,1,0:T(8,128)S(1)} fusion(f32[2,128,512]{2,1,0:T(8,128)S(1)} %convolution_subtract_fusion.1, f32[2,128,512]{2,1,0:T(8,128)S(1)} %convolution_add_fusion.1, f32[2,16,512]{2,1,0:T(8,128)S(1)} %copy.32, f32[2,16,512]{2,1,0:T(8,128)S(1)} %copy-done.5), kind=kOutput, calls=%fused_computation.39 | convolution fusion | flops 809369600 | bytes 1703936 | tf_op jit(solution)/shard_map/dot_general | solution.py:40
  287.7 5.0 %multiply_convert_fusion = (bf16[2,128,512]{2,1,0:T(8,128)(2,1)S(1)}, f32[2,128,512]{2,1,0:T(8,128)S(1)}) fusion(f32[2,128,512]{2,1,0:T(8,128)S(1)} %fusion.24, f32[2,128,512]{2,1,0:T(8,128)S(1)} %convolution_add_fusion.1, f32[2,128,512]{2,1,0:T(8,128)S(1)} %convolution_subtract_fusion.1, f32[2,16,512]{2,1,0:T(8,128)S(1)} %copy.32, ...), kind=kOutput, calls=%fused_computation.199 | convolution fusion | flops 809762816 | bytes 2490368 | tf_op jit(solution)/shard_map/dot_general | solution.py:40
  292.7 1.8 collective-permute-start.12
  294.5 5.2 %collective-permute-done.12 = bf16[2,128,512]{2,1,0:T(8,128)(2,1)S(1)} collective-permute-done((bf16[2,128,512]{2,1,0:T(8,128)(2,1)S(1)}, bf16[2,128,512]{2,1,0:T(8,128)(2,1)S(1)}, u32[]{:S(2)}, u32[]{:S(2)}) %collective-permute-start.12) | collective-permute-done | bytes 262176 | tf_op jit(solution)/shard_map/ppermute | solution.py:21
  300.2 6.1 %collective-permute-start.13 = (bf16[2,128,512]{2,1,0:T(8,128)(2,1)S(1)}, bf16[2,128,512]{2,1,0:T(8,128)(2,1)S(1)}, u32[]{:S(2)}, u32[]{:S(2)}) collective-permute-start(bf16[2,128,512]{2,1,0:T(8,128)(2,1)S(1)} %get-tuple-element.21), channel_id=1, source_target_pairs={{0,16},{16,0},{8,24},{24,8},{32,48},{48,32},{40,56},{56,40},{64,80... | collective-permute-start | bytes 786440 | tf_op jit(solution)/shard_map/ppermute | solution.py:21
  306.7 11.6 %collective-permute-done.13 = bf16[2,128,512]{2,1,0:T(8,128)(2,1)S(1)} collective-permute-done((bf16[2,128,512]{2,1,0:T(8,128)(2,1)S(1)}, bf16[2,128,512]{2,1,0:T(8,128)(2,1)S(1)}, u32[]{:S(2)}, u32[]{:S(2)}) %collective-permute-start.13) | collective-permute-done | bytes 262176 | tf_op jit(solution)/shard_map/ppermute | solution.py:21
  318.3 2.8 collective-permute-done.14
  321.6 5.8 %collective-permute-start.15 = (bf16[2,128,512]{2,1,0:T(8,128)(2,1)S(1)}, bf16[2,128,512]{2,1,0:T(8,128)(2,1)S(1)}, u32[]{:S(2)}, u32[]{:S(2)}) collective-permute-start(bf16[2,128,512]{2,1,0:T(8,128)(2,1)S(1)} %get-tuple-element.17), channel_id=1, source_target_pairs={{0,32},{32,0},{8,40},{40,8},{16,48},{48,16},{24,56},{56,24},{64,96... | collective-permute-start | bytes 786440 | tf_op jit(solution)/shard_map/ppermute | solution.py:21
  327.6 15.9 %collective-permute-done.15 = bf16[2,128,512]{2,1,0:T(8,128)(2,1)S(1)} collective-permute-done((bf16[2,128,512]{2,1,0:T(8,128)(2,1)S(1)}, bf16[2,128,512]{2,1,0:T(8,128)(2,1)S(1)}, u32[]{:S(2)}, u32[]{:S(2)}) %collective-permute-start.15) | collective-permute-done | bytes 262176 | tf_op jit(solution)/shard_map/ppermute | solution.py:21
  343.5 5.4 %collective-permute-done.16 = bf16[2,128,512]{2,1,0:T(8,128)(2,1)S(1)} collective-permute-done((bf16[2,128,512]{2,1,0:T(8,128)(2,1)S(1)}, bf16[2,128,512]{2,1,0:T(8,128)(2,1)S(1)}, u32[]{:S(2)}, u32[]{:S(2)}) %collective-permute-start.16) | collective-permute-done | bytes 262176 | tf_op jit(solution)/shard_map/ppermute | solution.py:21
  351.5 4.4 %collective-permute-done.17 = bf16[2,128,512]{2,1,0:T(8,128)(2,1)S(1)} collective-permute-done((bf16[2,128,512]{2,1,0:T(8,128)(2,1)S(1)}, bf16[2,128,512]{2,1,0:T(8,128)(2,1)S(1)}, u32[]{:S(2)}, u32[]{:S(2)}) %collective-permute-start.17) | collective-permute-done | bytes 262176 | tf_op jit(solution)/shard_map/ppermute | solution.py:21
  355.9 2.8 collective-permute-done.18
  359.2 11.5 %collective-permute-start.19 = (bf16[2,128,512]{2,1,0:T(8,128)(2,1)S(1)}, bf16[2,128,512]{2,1,0:T(8,128)(2,1)S(1)}, u32[]{:S(2)}, u32[]{:S(2)}) collective-permute-start(bf16[2,128,512]{2,1,0:T(8,128)(2,1)S(1)} %get-tuple-element.9), channel_id=1, source_target_pairs={{0,128},{128,0},{8,136},{136,8},{16,144},{144,16},{24,152},{152,24... | collective-permute-start | bytes 786440 | tf_op jit(solution)/shard_map/ppermute | solution.py:21
  370.8 6.3 %collective-permute-done.19 = bf16[2,128,512]{2,1,0:T(8,128)(2,1)S(1)} collective-permute-done((bf16[2,128,512]{2,1,0:T(8,128)(2,1)S(1)}, bf16[2,128,512]{2,1,0:T(8,128)(2,1)S(1)}, u32[]{:S(2)}, u32[]{:S(2)}) %collective-permute-start.19) | collective-permute-done | bytes 262176 | tf_op jit(solution)/shard_map/ppermute | solution.py:21
  377.0 2.8 collective-permute-done.20
  380.9 4.8 %convolution_convert_fusion = bf16[512,4096]{1,0:T(8,128)(2,1)} fusion(bf16[256,4096]{1,0:T(8,128)(2,1)} %all-gather.8.cloned.1.call-done, f32[512,3,256]{2,0,1:T(8,128)S(1)} %fusion.9, f32[256,512]{0,1:T(8,128)S(1)} %copy.39, f32[256]{0:T(256)S(1)} %copy-done.25), kind=kOutput, calls=%fused_computation.7 | convolution fusion | flops 1076494336 | bytes 8389632 | tf_op jit(solution)/shard_map/dot_general | solution.py:217
  385.8 42.0 %reduce-scatter.2.cloned.1.call-done = bf16[512,512]{1,0:T(8,128)(2,1)} async-done(((bf16[512,4096]{1,0:T(8,128)(2,1)}), bf16[512,512]{1,0:T(8,128)(2,1)}) %reduce-scatter.2.cloned.1.call-update) | async-done | bytes 524304 | tf_op jit(solution)/shard_map/reduce_scatter | solution.py:222
  (118 shorter events, 21.5 us)
Async XLA Ops:
  6.5 1.0 copy-start
  6.5 3.1 copy-start.4
  6.5 4.0 copy-start.6
  6.5 40.6 %all-gather.4.cloned.1.call-start = ((), (), s32[]{:S(2)}) async-start(), calls=%async_computation.1 | async-start | bytes 4718592 | tf_op jit(solution)/shard_map/all_gather | solution.py:180
  9.6 132.9 %all-gather.6.cloned.1.call-start = ((), (), s32[]{:S(2)}) async-start(), calls=%async_computation.2 | async-start | bytes 6488064 | tf_op jit(solution)/shard_map/all_gather | solution.py:184
  10.5 370.2 %all-gather.8.cloned.1.call-start = ((), (), s32[]{:S(2)}) async-start(), calls=%async_computation.3 | async-start | bytes 2162688 | tf_op jit(solution)/shard_map/all_gather | solution.py:219
  10.6 131.9 %copy-start.26 = (f32[4096]{0:T(1024)S(1)}, f32[4096]{0:T(1024)}, u32[]{:S(2)}) copy-start(f32[4096]{0:T(1024)} %param.11) | copy-start | bytes 49156
  150.0 7.7 %collective-permute-start = (bf16[6,3,256]{2,0,1:T(8,128)(2,1)S(1)}, bf16[6,3,256]{2,0,1:T(8,128)(2,1)S(1)}, u32[]{:S(2)}, u32[]{:S(2)}) collective-permute-start(bf16[6,3,256]{2,0,1:T(8,128)(2,1)S(1)} %slice.98), channel_id=1, source_target_pairs={{0,8},{8,16},{16,24},{24,32},{32,40},{40,48},{48,56},{56,64},{64,7... | collective-permute-start | bytes 27656 | tf_op jit(solution)/shard_map/ppermute | solution.py:27
  159.6 8.3 %collective-permute-start.1 = (bf16[2,128,512]{2,1,0:T(8,128)(2,1)S(1)}, bf16[2,128,512]{2,1,0:T(8,128)(2,1)}, u32[]{:S(2)}, u32[]{:S(2)}) collective-permute-start(bf16[2,128,512]{2,1,0:T(8,128)(2,1)S(1)} %fusion.123), channel_id=1, source_target_pairs={{0,128},{128,0},{8,136},{136,8},{16,144},{144,16},{24,152},{152,24... | collective-permute-start | bytes 786440 | tf_op jit(solution)/shard_map/ppermute | solution.py:21
  160.3 10.6 %collective-permute-start.2 = (bf16[2,128,512]{2,1,0:T(8,128)(2,1)S(1)}, bf16[2,128,512]{2,1,0:T(8,128)(2,1)}, u32[]{:S(2)}, u32[]{:S(2)}) collective-permute-start(bf16[2,128,512]{2,1,0:T(8,128)(2,1)S(1)} %fusion.122), channel_id=1, source_target_pairs={{0,128},{128,0},{8,136},{136,8},{16,144},{144,16},{24,152},{152,24... | collective-permute-start | bytes 786440 | tf_op jit(solution)/shard_map/ppermute | solution.py:21
  163.4 264.5 %reduce-scatter.2.cloned.1.call-start = ((), (), s32[]{:S(2)}) async-start(), calls=%async_computation.4 | async-start | bytes 4718592 | tf_op jit(solution)/shard_map/reduce_scatter | solution.py:222
  163.6 20.1 %copy-start.7 = (f32[512]{0:T(512)}, f32[512]{0:T(512)S(1)}, u32[]{:S(2)}) copy-start(f32[512]{0:T(512)S(1)} %get-tuple-element.94) | copy-start | bytes 6148
  163.6 20.1 %copy-start.9 = (f32[512]{0:T(512)}, f32[512]{0:T(512)S(1)}, u32[]{:S(2)}) copy-start(f32[512]{0:T(512)S(1)} %get-tuple-element.95) | copy-start | bytes 6148
  173.3 6.9 %collective-permute-start.3 = (bf16[2,128,512]{2,1,0:T(8,128)(2,1)}, bf16[2,128,512]{2,1,0:T(8,128)(2,1)S(1)}, u32[]{:S(2)}, u32[]{:S(2)}) collective-permute-start(bf16[2,128,512]{2,1,0:T(8,128)(2,1)} %get-tuple-element.35), channel_id=1, source_target_pairs={{0,64},{64,0},{8,72},{72,8},{16,80},{80,16},{24,88},{88,24},{32,96... | collective-permute-start | bytes 786440 | tf_op jit(solution)/shard_map/ppermute | solution.py:21
  174.2 8.8 %collective-permute-start.4 = (bf16[2,128,512]{2,1,0:T(8,128)(2,1)}, bf16[2,128,512]{2,1,0:T(8,128)(2,1)S(1)}, u32[]{:S(2)}, u32[]{:S(2)}) collective-permute-start(bf16[2,128,512]{2,1,0:T(8,128)(2,1)} %get-tuple-element.57), channel_id=1, source_target_pairs={{0,64},{64,0},{8,72},{72,8},{16,80},{80,16},{24,88},{88,24},{32,96... | collective-permute-start | bytes 786440 | tf_op jit(solution)/shard_map/ppermute | solution.py:21
  186.0 15.6 %collective-permute-start.5 = (bf16[2,128,512]{2,1,0:T(8,128)(2,1)}, bf16[2,128,512]{2,1,0:T(8,128)(2,1)S(1)}, u32[]{:S(2)}, u32[]{:S(2)}) collective-permute-start(bf16[2,128,512]{2,1,0:T(8,128)(2,1)} %get-tuple-element.31), channel_id=1, source_target_pairs={{0,32},{32,0},{8,40},{40,8},{16,48},{48,16},{24,56},{56,24},{64,96... | collective-permute-start | bytes 786440 | tf_op jit(solution)/shard_map/ppermute | solution.py:21
  188.4 17.7 %collective-permute-start.6 = (bf16[2,128,512]{2,1,0:T(8,128)(2,1)}, bf16[2,128,512]{2,1,0:T(8,128)(2,1)S(1)}, u32[]{:S(2)}, u32[]{:S(2)}) collective-permute-start(bf16[2,128,512]{2,1,0:T(8,128)(2,1)} %get-tuple-element.55), channel_id=1, source_target_pairs={{0,32},{32,0},{8,40},{40,8},{16,48},{48,16},{24,56},{56,24},{64,96... | collective-permute-start | bytes 786440 | tf_op jit(solution)/shard_map/ppermute | solution.py:21
  192.0 16.5 %copy-start.11 = (f32[512]{0:T(512)}, f32[512]{0:T(512)S(1)}, u32[]{:S(2)}) copy-start(f32[512]{0:T(512)S(1)} %get-tuple-element.96) | copy-start | bytes 6148
  192.0 16.5 %copy-start.13 = (f32[512]{0:T(512)}, f32[512]{0:T(512)S(1)}, u32[]{:S(2)}) copy-start(f32[512]{0:T(512)S(1)} %get-tuple-element.97) | copy-start | bytes 6148
  206.1 8.4 %copy-start.23 = (f32[16,16]{1,0:T(8,128)S(1)}, f32[16,16]{1,0:T(8,128)}, u32[]{:S(2)}) copy-start(f32[16,16]{1,0:T(8,128)} %param.14) | copy-start | bytes 3076
  208.5 18.8 %collective-permute-start.7 = (bf16[2,128,512]{2,1,0:T(8,128)(2,1)}, bf16[2,128,512]{2,1,0:T(8,128)(2,1)S(1)}, u32[]{:S(2)}, u32[]{:S(2)}) collective-permute-start(bf16[2,128,512]{2,1,0:T(8,128)(2,1)} %get-tuple-element.27), channel_id=1, source_target_pairs={{0,16},{16,0},{8,24},{24,8},{32,48},{48,32},{40,56},{56,40},{64,80... | collective-permute-start | bytes 786440 | tf_op jit(solution)/shard_map/ppermute | solution.py:21
  214.3 15.8 %collective-permute-start.8 = (bf16[2,128,512]{2,1,0:T(8,128)(2,1)}, bf16[2,128,512]{2,1,0:T(8,128)(2,1)S(1)}, u32[]{:S(2)}, u32[]{:S(2)}) collective-permute-start(bf16[2,128,512]{2,1,0:T(8,128)(2,1)} %get-tuple-element.53), channel_id=1, source_target_pairs={{0,16},{16,0},{8,24},{24,8},{32,48},{48,32},{40,56},{56,40},{64,80... | collective-permute-start | bytes 786440 | tf_op jit(solution)/shard_map/ppermute | solution.py:21
  214.5 18.7 %copy-start.15 = (f32[512]{0:T(512)}, f32[512]{0:T(512)S(1)}, u32[]{:S(2)}) copy-start(f32[512]{0:T(512)S(1)} %get-tuple-element.98) | copy-start | bytes 6148
  214.5 18.7 %copy-start.17 = (f32[512]{0:T(512)}, f32[512]{0:T(512)S(1)}, u32[]{:S(2)}) copy-start(f32[512]{0:T(512)S(1)} %get-tuple-element.99) | copy-start | bytes 6148
  230.8 4.4 %copy-start.19 = (f32[1024]{0:T(1024)S(1)}, f32[1024]{0:T(1024)}, u32[]{:S(2)}) copy-start(f32[1024]{0:T(1024)} %get-tuple-element.76) | copy-start | bytes 12292
  230.8 4.4 %copy-start.20 = (f32[1024]{0:T(1024)S(1)}, f32[1024]{0:T(1024)}, u32[]{:S(2)}) copy-start(f32[1024]{0:T(1024)} %get-tuple-element.77) | copy-start | bytes 12292
  230.8 4.4 %copy-start.21 = (f32[1024]{0:T(1024)S(1)}, f32[1024]{0:T(1024)}, u32[]{:S(2)}) copy-start(f32[1024]{0:T(1024)} %get-tuple-element.78) | copy-start | bytes 12292
  230.8 4.4 %copy-start.22 = (f32[1024]{0:T(1024)S(1)}, f32[1024]{0:T(1024)}, u32[]{:S(2)}) copy-start(f32[1024]{0:T(1024)} %get-tuple-element.79) | copy-start | bytes 12292
  230.8 4.4 %copy-start.24 = (f32[16,16]{1,0:T(8,128)S(1)}, f32[16,16]{1,0:T(8,128)}, u32[]{:S(2)}) copy-start(f32[16,16]{1,0:T(8,128)} %param.15) | copy-start | bytes 3076
  233.2 11.2 %collective-permute-start.10 = (bf16[2,128,512]{2,1,0:T(8,128)(2,1)}, bf16[2,128,512]{2,1,0:T(8,128)(2,1)S(1)}, u32[]{:S(2)}, u32[]{:S(2)}) collective-permute-start(bf16[2,128,512]{2,1,0:T(8,128)(2,1)} %get-tuple-element.51), channel_id=1, source_target_pairs={{0,8},{8,0},{16,24},{24,16},{32,40},{40,32},{48,56},{56,48},{64,72... | collective-permute-start | bytes 786440 | tf_op jit(solution)/shard_map/ppermute | solution.py:21
  234.5 15.0 %collective-permute-start.9 = (bf16[2,128,512]{2,1,0:T(8,128)(2,1)}, bf16[2,128,512]{2,1,0:T(8,128)(2,1)}, u32[]{:S(2)}, u32[]{:S(2)}) collective-permute-start(bf16[2,128,512]{2,1,0:T(8,128)(2,1)} %get-tuple-element.23), channel_id=1, source_target_pairs={{0,8},{8,0},{16,24},{24,16},{32,40},{40,32},{48,56},{56,48},{64,72... | collective-permute-start | bytes 786440 | tf_op jit(solution)/shard_map/ppermute | solution.py:21
  266.7 5.5 %copy-start.5 = (f32[2,16,512]{2,1,0:T(8,128)S(1)}, f32[2,16,512]{2,1,0:T(8,128)}, u32[]{:S(2)}) copy-start(f32[2,16,512]{2,1,0:T(8,128)} %copy.31) | copy-start | bytes 196612
  282.1 12.4 %collective-permute-start.11 = (bf16[2,128,512]{2,1,0:T(8,128)(2,1)S(1)}, bf16[2,128,512]{2,1,0:T(8,128)(2,1)S(1)}, u32[]{:S(2)}, u32[]{:S(2)}) collective-permute-start(bf16[2,128,512]{2,1,0:T(8,128)(2,1)S(1)} %get-tuple-element.82), channel_id=1, source_target_pairs={{0,8},{8,0},{16,24},{24,16},{32,40},{40,32},{48,56},{56,48},{64,72... | collective-permute-start | bytes 786440 | tf_op jit(solution)/shard_map/ppermute | solution.py:21
  292.7 7.1 %collective-permute-start.12 = (bf16[2,128,512]{2,1,0:T(8,128)(2,1)S(1)}, bf16[2,128,512]{2,1,0:T(8,128)(2,1)S(1)}, u32[]{:S(2)}, u32[]{:S(2)}) collective-permute-start(bf16[2,128,512]{2,1,0:T(8,128)(2,1)S(1)} %get-tuple-element.80), channel_id=1, source_target_pairs={{0,8},{8,0},{16,24},{24,16},{32,40},{40,32},{48,56},{56,48},{64,72... | collective-permute-start | bytes 786440 | tf_op jit(solution)/shard_map/ppermute | solution.py:21
  299.8 21.4 %copy-start.16 = (f32[512]{0:T(512)S(1)}, f32[512]{0:T(512)}, u32[]{:S(2)}) copy-start(f32[512]{0:T(512)} %copy-done.15) | copy-start | bytes 6148
  299.8 21.4 %copy-start.18 = (f32[512]{0:T(512)S(1)}, f32[512]{0:T(512)}, u32[]{:S(2)}) copy-start(f32[512]{0:T(512)} %copy-done.17) | copy-start | bytes 6148
  300.2 18.1 %collective-permute-start.13 = (bf16[2,128,512]{2,1,0:T(8,128)(2,1)S(1)}, bf16[2,128,512]{2,1,0:T(8,128)(2,1)S(1)}, u32[]{:S(2)}, u32[]{:S(2)}) collective-permute-start(bf16[2,128,512]{2,1,0:T(8,128)(2,1)S(1)} %get-tuple-element.21), channel_id=1, source_target_pairs={{0,16},{16,0},{8,24},{24,8},{32,48},{48,32},{40,56},{56,40},{64,80... | collective-permute-start | bytes 786440 | tf_op jit(solution)/shard_map/ppermute | solution.py:21
  306.4 14.7 %collective-permute-start.14 = (bf16[2,128,512]{2,1,0:T(8,128)(2,1)S(1)}, bf16[2,128,512]{2,1,0:T(8,128)(2,1)S(1)}, u32[]{:S(2)}, u32[]{:S(2)}) collective-permute-start(bf16[2,128,512]{2,1,0:T(8,128)(2,1)S(1)} %get-tuple-element.39), channel_id=1, source_target_pairs={{0,16},{16,0},{8,24},{24,8},{32,48},{48,32},{40,56},{56,40},{64,80... | collective-permute-start | bytes 786440 | tf_op jit(solution)/shard_map/ppermute | solution.py:21
  321.1 27.8 %copy-start.12 = (f32[512]{0:T(512)S(1)}, f32[512]{0:T(512)}, u32[]{:S(2)}) copy-start(f32[512]{0:T(512)} %copy-done.11) | copy-start | bytes 6148
  321.1 27.8 %copy-start.14 = (f32[512]{0:T(512)S(1)}, f32[512]{0:T(512)}, u32[]{:S(2)}) copy-start(f32[512]{0:T(512)} %copy-done.13) | copy-start | bytes 6148
  321.6 21.9 %collective-permute-start.15 = (bf16[2,128,512]{2,1,0:T(8,128)(2,1)S(1)}, bf16[2,128,512]{2,1,0:T(8,128)(2,1)S(1)}, u32[]{:S(2)}, u32[]{:S(2)}) collective-permute-start(bf16[2,128,512]{2,1,0:T(8,128)(2,1)S(1)} %get-tuple-element.17), channel_id=1, source_target_pairs={{0,32},{32,0},{8,40},{40,8},{16,48},{48,16},{24,56},{56,24},{64,96... | collective-permute-start | bytes 786440 | tf_op jit(solution)/shard_map/ppermute | solution.py:21
  327.4 21.5 %collective-permute-start.16 = (bf16[2,128,512]{2,1,0:T(8,128)(2,1)S(1)}, bf16[2,128,512]{2,1,0:T(8,128)(2,1)S(1)}, u32[]{:S(2)}, u32[]{:S(2)}) collective-permute-start(bf16[2,128,512]{2,1,0:T(8,128)(2,1)S(1)} %get-tuple-element.47), channel_id=1, source_target_pairs={{0,32},{32,0},{8,40},{40,8},{16,48},{48,16},{24,56},{56,24},{64,96... | collective-permute-start | bytes 786440 | tf_op jit(solution)/shard_map/ppermute | solution.py:21
  348.9 9.8 %copy-start.8 = (f32[512]{0:T(512)S(1)}, f32[512]{0:T(512)}, u32[]{:S(2)}) copy-start(f32[512]{0:T(512)} %copy-done.7) | copy-start | bytes 6148
  348.9 9.8 %copy-start.10 = (f32[512]{0:T(512)S(1)}, f32[512]{0:T(512)}, u32[]{:S(2)}) copy-start(f32[512]{0:T(512)} %copy-done.9) | copy-start | bytes 6148
  349.4 6.5 %collective-permute-start.17 = (bf16[2,128,512]{2,1,0:T(8,128)(2,1)S(1)}, bf16[2,128,512]{2,1,0:T(8,128)(2,1)S(1)}, u32[]{:S(2)}, u32[]{:S(2)}) collective-permute-start(bf16[2,128,512]{2,1,0:T(8,128)(2,1)S(1)} %get-tuple-element.13), channel_id=1, source_target_pairs={{0,64},{64,0},{8,72},{72,8},{16,80},{80,16},{24,88},{88,24},{32,96... | collective-permute-start | bytes 786440 | tf_op jit(solution)/shard_map/ppermute | solution.py:21
  351.0 7.8 %collective-permute-start.18 = (bf16[2,128,512]{2,1,0:T(8,128)(2,1)S(1)}, bf16[2,128,512]{2,1,0:T(8,128)(2,1)S(1)}, u32[]{:S(2)}, u32[]{:S(2)}) collective-permute-start(bf16[2,128,512]{2,1,0:T(8,128)(2,1)S(1)} %get-tuple-element.45), channel_id=1, source_target_pairs={{0,64},{64,0},{8,72},{72,8},{16,80},{80,16},{24,88},{88,24},{32,96... | collective-permute-start | bytes 786440 | tf_op jit(solution)/shard_map/ppermute | solution.py:21
  359.2 17.9 %collective-permute-start.19 = (bf16[2,128,512]{2,1,0:T(8,128)(2,1)S(1)}, bf16[2,128,512]{2,1,0:T(8,128)(2,1)S(1)}, u32[]{:S(2)}, u32[]{:S(2)}) collective-permute-start(bf16[2,128,512]{2,1,0:T(8,128)(2,1)S(1)} %get-tuple-element.9), channel_id=1, source_target_pairs={{0,128},{128,0},{8,136},{136,8},{16,144},{144,16},{24,152},{152,24... | collective-permute-start | bytes 786440 | tf_op jit(solution)/shard_map/ppermute | solution.py:21
  370.7 9.2 %collective-permute-start.20 = (bf16[2,128,512]{2,1,0:T(8,128)(2,1)S(1)}, bf16[2,128,512]{2,1,0:T(8,128)(2,1)S(1)}, u32[]{:S(2)}, u32[]{:S(2)}) collective-permute-start(bf16[2,128,512]{2,1,0:T(8,128)(2,1)S(1)} %get-tuple-element.43), channel_id=1, source_target_pairs={{0,128},{128,0},{8,136},{136,8},{16,144},{144,16},{24,152},{152,24... | collective-permute-start | bytes 786440 | tf_op jit(solution)/shard_map/ppermute | solution.py:21
  (4 other events, 2.8 us)
Sparse Core Ops, SparseCore 0:
  9.7 37.4 all-gather.3
  49.6 92.8 all-gather.5
  163.5 95.5 all-gather.7
  385.9 41.8 reduce-scatter.1
where the time goes:
time: 444 us; the launch traced here: 435 us
  waiting for transfers between devices  287 us (65%)
  matrix products  55.7 us (13%)
  starting transfers between devices  52 us (12%)
  other arithmetic  19.3 us (4%)
  between operations  14.2 us (3%)
  local copies, waits for them, and re-layouts  6.88 us (2%)
    ppermute x20, waiting for transfers between devices, from_partner(): return lax.ppermute(block, axis, route)  112 us
    all_gather x1, waiting for transfers between devices, body(): block_piece = lax.all_gather(in_weight, 'ctx', axis=0, tiled=True)  92.2 us
    ppermute x20, starting transfers between devices, from_partner(): return lax.ppermute(block, axis, route)  47.7 us
    reduce_scatter x1, waiting for transfers between devices, body(): lax.psum_scatter(partial_out.astype(jnp.bfloat16), 'fsdp', scatter_dimens...  42 us
    all_gather x1, waiting for transfers between devices, body(): features = lax.all_gather(own_columns, 'fsdp', axis=1, tiled=True)  36.6 us
    dot_general x2, matrix products, direct_dft(): jnp.dot(real_part, cosine_table, precision=highest_precision)  10.4 us
    dot_general x2, matrix products, direct_dft(): jnp.dot(imag_part, sine_table, precision=highest_precision)  10.3 us
    dot_general x2, matrix products, direct_dft(): jnp.dot(real_part, sine_table, precision=highest_precision)  10.3 us
  transfers between devices with their start and end apart: 25, of which 23 were waited for; matrix products, arithmetic and copies ran while one was open for 14% of the time, Pallas kernels for 0%

commit v1 on v0

v1 whole, which is shorter than its diff:
```python
import jax
import jax.numpy as jnp
from jax import lax
from jax.sharding import PartitionSpec as P

GROUP = 16
CHUNK = 128


def body(
    tokens,
    embedding,
    norm_gain,
    in_weight,
    short_taps,
    decay_rates,
    residue,
    skip_weight,
    out_weight,
):
    count = tokens.shape[0]
    vocab = embedding.shape[0]
    rows = in_weight.shape[0]
    channels = in_weight.shape[2]
    width = norm_gain.shape[0]
    own = lax.axis_index("ctx")
    column = lax.axis_index("fsdp")
    ctx_count = lax.axis_size("ctx")
    fsdp_count = lax.axis_size("fsdp")
    share = ctx_count // fsdp_count

    route = [
        (i * fsdp_count + j, (share * j + i % share) * fsdp_count + i // share)
        for i in range(ctx_count)
        for j in range(fsdp_count)
    ]
    swapped = lax.ppermute(out_weight, ("ctx", "fsdp"), route)
    out_blocks = lax.all_gather(swapped, "ctx", axis=0)
    out_panel = (
        out_blocks.reshape(fsdp_count, share, channels, rows)
        .transpose(0, 2, 1, 3)
        .reshape(fsdp_count * channels, share * rows)
    )

    piece = lax.dynamic_slice(embedding, (0, own % share * rows), (vocab, rows))
    piece = jnp.where(column == own // share, piece, jnp.zeros_like(piece))
    piece = lax.psum(piece, "fsdp").astype(jnp.float32)
    gain = lax.dynamic_slice(norm_gain, (own * rows,), (rows,))
    squares = lax.psum(jnp.sum(piece * piece, axis=1), "ctx")
    scale = lax.rsqrt(squares / width + 1e-05)
    panel = in_weight.reshape(rows, 3 * channels)
    partial_table = jnp.dot(
        (piece * gain).astype(jnp.bfloat16), panel, preferred_element_type=jnp.float32
    ).astype(jnp.bfloat16)
    table = lax.psum_scatter(partial_table, "ctx", scatter_dimension=0, tiled=True)
    table = lax.all_gather(table, "ctx", axis=0, tiled=True)
    table = (table.astype(jnp.float32) * scale[:, None]).astype(jnp.bfloat16)

    reach = short_taps.shape[0] - 1
    before = lax.ppermute(
        tokens[count - reach :], "ctx", [(k, k + 1) for k in range(ctx_count - 1)]
    )
    before = jnp.where(own > 0, before, -1)
    wanted = jnp.concatenate([before, tokens])
    one_hot = (wanted[:, None] == jnp.arange(vocab)[None, :]).astype(jnp.bfloat16)
    projected = jnp.dot(one_hot, table, preferred_element_type=jnp.float32)
    taps = short_taps.reshape(reach + 1, 3 * channels)
    short = jnp.zeros((count, 3 * channels), jnp.float32)
    for lag in range(reach + 1):
        short = short + taps[lag] * projected[reach - lag : reach - lag + count]
    short = short.T
    queries = short[:channels]
    driving = short[channels : 2 * channels] * short[2 * channels :]

    groups = channels // GROUP
    chunks = count // CHUNK
    high = lax.Precision.HIGHEST
    steps = jnp.arange(CHUNK, dtype=jnp.float32)
    lag_grid = steps[None, :] - steps[:, None]
    rates = decay_rates.T
    filters = jnp.sum(
        residue.T[:, :, None] * jnp.exp(-rates[:, :, None] * steps), axis=1
    )
    index = jnp.maximum(lag_grid, 0).astype(jnp.int32)
    toeplitz = jnp.where(lag_grid >= 0, jnp.take(filters, index, axis=1), 0.0)
    blocks = driving.reshape(groups, GROUP, chunks, CHUNK)
    inside = jnp.einsum("gcks,gst->gckt", blocks, toeplitz, precision=high)
    to_end = jnp.exp(-rates[:, :, None] * (CHUNK - 1 - steps))
    ends = jnp.einsum("gcks,gms->kgcm", blocks, to_end, precision=high)
    over_chunk = jnp.exp(-rates * CHUNK)[:, None, :]
    total = ends[0]
    for k in range(1, chunks):
        total = over_chunk * total + ends[k]
    totals = lax.all_gather(total, "ctx", axis=0)
    distance = (own - 1 - jnp.arange(ctx_count)).astype(jnp.float32)
    carried = jnp.where(
        distance[:, None, None] >= 0,
        jnp.exp(-rates[None] * count * jnp.maximum(distance, 0)[:, None, None]),
        0.0,
    )
    state = jnp.sum(carried[:, :, None, :] * totals, axis=0)
    states = [state]
    for k in range(1, chunks):
        states.append(over_chunk * states[-1] + ends[k - 1])
    from_end = residue.T[:, :, None] * jnp.exp(-rates[:, :, None] * (steps + 1))
    outside = jnp.einsum("kgcm,gmt->gckt", jnp.stack(states), from_end, precision=high)
    convolved = (inside + outside).reshape(channels, count)
    response = convolved + skip_weight[:, None] * driving
    gated = (queries * response).astype(jnp.bfloat16).T
    every = lax.all_gather(gated, "fsdp", axis=1, tiled=True)
    return jnp.dot(every, out_panel, preferred_element_type=jnp.float32).astype(
        jnp.bfloat16
    )


def solution(mesh):
    placed = (
        P("ctx"),
        P(None, "fsdp"),
        P(),
        P("ctx", None, "fsdp"),
        P(None, None, "fsdp"),
        P(None, "fsdp"),
        P(None, "fsdp"),
        P("fsdp"),
        P("fsdp", "ctx"),
    )
    return jax.shard_map(
        body, mesh=mesh, in_specs=placed, out_specs=P("ctx", "fsdp"), check_vma=False
    )
```

time: 444 us -> 450 us (1.014)
  the two profiles are of different devices: /device:TPU:16 before, /device:TPU:1 now
where the time goes in v1:
time: 450 us
  waiting for transfers between devices  190 us (42%)
  blocking collectives  143 us (32%)
  local copies, waits for them, and re-layouts  71 us (16%)
  between operations  13.4 us (3%)
  matrix products  13.2 us (3%)
  starting transfers between devices  12.7 us (3%)
  other arithmetic  6.03 us (1%)
    reduce_scatter x1, waiting for transfers between devices, body(): lax.psum_scatter(partial_table, 'ctx', scatter_dimension=0, tiled=True)  77.1 us
    psum x1, waiting for transfers between devices, body(): piece = lax.psum(piece, 'fsdp').astype(jnp.float32)  65.6 us
    gather x2, local copies, waits for them, and re-layouts, body(): toeplitz = jnp.where(lag_grid >= 0, jnp.take(filters, index, axis=1), 0.0)  59.7 us
    psum x1, blocking collectives, body(): squares = lax.psum(jnp.sum(piece * piece, axis=1), 'ctx')  59.5 us
    all_gather x1, blocking collectives, body(): totals = lax.all_gather(total, 'ctx', axis=0)  47 us
    all_gather x1, waiting for transfers between devices, body(): every = lax.all_gather(gated, 'fsdp', axis=1, tiled=True)  45.9 us
    all_gather x1, blocking collectives, body(): table = lax.all_gather(table, 'ctx', axis=0, tiled=True)  36.7 us
    ppermute x1, starting transfers between devices, body(): swapped = lax.ppermute(out_weight, ('ctx', 'fsdp'), route)  9.4 us
  transfers between devices with their start and end apart: 6, of which 4 were waited for; matrix products, arithmetic and copies ran while one was open for 18% of the time, Pallas kernels for 0%

profile of v1, /device:TPU:1, one launch (start us, length us, event | category | flops | bytes accessed | tf_op | source)
XLA Modules:
  0.0 449.5 jit_solution(13309358924967620183)
XLA Ops:
  6.6 1.6 dynamic-slice_select_fusion
  8.2 0.0 reduce-scatter.2.cloned.1.call-start
  8.3 1.1 copy.32
  9.4 0.8 dynamic_slice.7
  10.1 65.6 %all-reduce.2.cloned.1.call-done = bf16[512,128]{1,0:T(8,128)(2,1)} async-done(((bf16[512,128]{1,0:T(8,128)(2,1)}), bf16[512,128]{1,0:T(8,128)(2,1)}) %all-reduce.2.cloned.1.call-update) | async-done | bytes 131088 | tf_op jit(solution)/shard_map/psum | solution.py:47
  75.7 2.2 convolution_convert_fusion
  78.0 0.1 slice.77
  78.1 3.2 collective-permute-start
  81.2 9.4 %collective-permute-start.1 = (bf16[256,128]{1,0:T(8,128)(2,1)S(1)}, bf16[256,128]{1,0:T(8,128)(2,1)S(1)}, u32[]{:S(2)}, u32[]{:S(2)}) collective-permute-start(bf16[256,128]{1,0:T(8,128)(2,1)S(1)} %copy-done.7), channel_id=1, source_target_pairs={{0,0},{1,32},{2,64},{3,96},{4,128},{5,160},{6,192},{7,224},{8,8},{... | collective-permute-start | bytes 196616 | tf_op jit(solution)/shard_map/ppermute | solution.py:37
  90.7 0.1 copy.35
  90.8 0.1 copy.39
  90.8 0.1 copy.34
  90.9 0.1 slice_reduce_fusion.6
  91.0 0.1 multiply_reduce_fusion.1
  91.2 0.1 exponential_select_fusion
  91.3 1.2 collective-permute-done.1
  92.6 0.6 copy-done.1
  93.2 0.0 all-gather.4.cloned.1.call-start
  93.4 0.1 copy.40
  93.5 0.1 copy.36
  93.6 54.4 %gather_fusion = f32[16384,16]{1,0:T(8,128)} fusion(f32[16,128]{0,1:T(8,128)S(1)} %copy.36, s32[16384]{0:T(1024)S(1)} %fusion.40), kind=kCustom, calls=%fused_computation | custom fusion | bytes 2162688 | tf_op jit(solution)/shard_map/jit(_take)/gather | solution.py:85
  148.0 5.3 %copy.37 = f32[128,128,16]{1,0,2:T(8,128)S(1)} copy(f32[128,128,16]{2,1,0:T(8,128)} %bitcast.56) | data formatting | bytes 2097152 | tf_op jit(solution)/shard_map/jit(_take)/gather | solution.py:85
  153.3 0.1 fusion.46
  153.4 0.1 pad_add_fusion
  153.4 0.1 fusion.28
  153.6 59.5 %psum.15 = f32[512]{0:T(512)S(1)} all-reduce(f32[512]{0:T(512)S(1)} %fusion.28), channel_id=1, replica_groups=mesh['ctx'=32,'fsdp'=8] {'ctx'}, use_global_device_ids=true, to_apply=%region_3.4 | all-reduce | flops 512 | bytes 4096 | tf_op jit(solution)/shard_map/psum | solution.py:49
  213.0 77.1 %reduce-scatter.2.cloned.1.call-done = bf16[16,768]{1,0:T(8,128)(2,1)} async-done(((bf16[512,768]{1,0:T(8,128)(2,1)}), bf16[16,768]{1,0:T(8,128)(2,1)}) %reduce-scatter.2.cloned.1.call-update) | async-done | bytes 24592 | tf_op jit(solution)/shard_map/reduce_scatter | solution.py:55
  290.1 36.7 %all_gather.16 = bf16[512,768]{1,0:T(8,128)(2,1)S(1)} all-gather(bf16[16,768]{1,0:T(8,128)(2,1)} %reduce-scatter.2.cloned.1.call-done), channel_id=1, replica_groups=mesh['ctx'=32,'fsdp'=8] {'ctx'}, dimensions={0}, use_global_device_ids=true | all-gather | bytes 811008 | tf_op jit(solution)/shard_map/all_gather | solution.py:56
  326.8 0.7 fusion.7
  327.6 1.3 fusion.1
  328.9 0.1 slice_multiply_fusion.7
  329.0 1.0 copy.33
  329.9 1.2 reshape.120
  331.2 3.8 convolution_bitcast_fusion.1
  335.0 0.1 slice_add_fusion
  335.1 47.0 %all_gather.17 = f32[32,16,16,16]{2,3,0,1:T(8,128)S(1)} all-gather(f32[1,16,16,16]{2,3,0,1:T(8,128)S(1)} %slice_add_fusion), channel_id=1, replica_groups=mesh['ctx'=32,'fsdp'=8] {'ctx'}, dimensions={0}, use_global_device_ids=true | all-gather | bytes 540672 | tf_op jit(solution)/shard_map/all_gather | solution.py:94
  382.1 1.4 multiply_reduce_fusion
  383.5 0.1 multiply_add_fusion
  383.6 1.1 convolution_bitcast_fusion
  384.7 1.1 convolution_add_fusion
  385.9 0.2 copy.43
  386.1 0.2 copy.44
  386.3 0.2 copy-done.6
  386.5 0.8 fusion.29
  387.4 3.4 copy.45
  390.8 2.0 copy.51
  392.8 45.9 %all-gather.4.cloned.1.call-done = bf16[512,2048]{1,0:T(8,128)(2,1)} async-done(((bf16[512,256]{1,0:T(8,128)(2,1)}), bf16[512,2048]{1,0:T(8,128)(2,1)}) %all-gather.4.cloned.1.call-update) | async-done | bytes 2097168 | tf_op jit(solution)/shard_map/all_gather | solution.py:110
  438.7 4.3 convolution_convert_fusion.1
  (39 shorter events, 0.4 us)
Async XLA Ops:
  6.5 71.4 %copy-start.5 = (s32[512]{0:T(512)S(1)}, s32[512]{0:T(512)}, u32[]{:S(2)}) copy-start(s32[512]{0:T(512)} %param.9) | copy-start | bytes 6148
  6.5 74.7 %copy-start.7 = (bf16[256,128]{1,0:T(8,128)(2,1)S(1)}, bf16[256,128]{1,0:T(8,128)(2,1)}, u32[]{:S(2)}) copy-start(bf16[256,128]{1,0:T(8,128)(2,1)} %param.17) | copy-start | bytes 196612
  6.5 84.1 %copy-start.2 = (f32[16,16]{1,0:T(8,128)S(1)}, f32[16,16]{1,0:T(8,128)}, u32[]{:S(2)}) copy-start(f32[16,16]{1,0:T(8,128)} %param.14) | copy-start | bytes 3076
  6.5 84.3 %copy-start.4 = (f32[16,16]{1,0:T(8,128)S(1)}, f32[16,16]{1,0:T(8,128)}, u32[]{:S(2)}) copy-start(f32[16,16]{1,0:T(8,128)} %param.15) | copy-start | bytes 3076
  6.5 84.4 %copy-start.3 = (f32[7,3,256]{2,0,1:T(8,128)S(1)}, f32[7,3,256]{2,0,1:T(8,128)}, u32[]{:S(2)}) copy-start(f32[7,3,256]{2,0,1:T(8,128)} %param.13) | copy-start | bytes 64516
  6.5 69.2 %all-reduce.2.cloned.1.call-start = ((), (), s32[]{:S(2)}) async-start(), calls=%async_computation.1 | async-start | bytes 262144 | tf_op jit(solution)/shard_map/psum | solution.py:47
  8.2 281.9 %reduce-scatter.2.cloned.1.call-start = ((), (), s32[]{:S(2)}) async-start(), calls=%async_computation.2 | async-start | bytes 811008 | tf_op jit(solution)/shard_map/reduce_scatter | solution.py:55
  77.9 309.5 %all-gather.6.cloned.1.call-start = ((), (), s32[]{:S(2)}) async-start(), calls=%async_computation.4 | async-start | bytes 2162688 | tf_op jit(solution)/shard_map/all_gather | solution.py:38
  78.1 75.3 %collective-permute-start = (s32[6]{0:T(128)S(1)}, s32[6]{0:T(128)S(1)}, u32[]{:S(2)}, u32[]{:S(2)}) collective-permute-start(s32[6]{0:T(128)S(1)} %slice.77), channel_id=1, source_target_pairs={{0,8},{8,16},{16,24},{24,32},{32,40},{40,48},{48,56},{56,64},{64,7... | collective-permute-start | bytes 80 | tf_op jit(solution)/shard_map/ppermute | solution.py:60
  81.2 11.3 %collective-permute-start.1 = (bf16[256,128]{1,0:T(8,128)(2,1)S(1)}, bf16[256,128]{1,0:T(8,128)(2,1)S(1)}, u32[]{:S(2)}, u32[]{:S(2)}) collective-permute-start(bf16[256,128]{1,0:T(8,128)(2,1)S(1)} %copy-done.7), channel_id=1, source_target_pairs={{0,0},{1,32},{2,64},{3,96},{4,128},{5,160},{6,192},{7,224},{8,8},{... | collective-permute-start | bytes 196616 | tf_op jit(solution)/shard_map/ppermute | solution.py:37
  92.6 0.6 copy-start.1
  93.2 345.5 %all-gather.4.cloned.1.call-start = ((), (), s32[]{:S(2)}) async-start(), calls=%async_computation.3 | async-start | bytes 2359296 | tf_op jit(solution)/shard_map/all_gather | solution.py:110
  148.0 5.5 %copy-start = (bf16[512,128]{1,0:T(8,128)(2,1)S(1)}, bf16[512,128]{1,0:T(8,128)(2,1)}, u32[]{:S(2)}) copy-start(bf16[512,128]{1,0:T(8,128)(2,1)} %all-reduce.2.cloned.1.call-done) | copy-start | bytes 393220
  385.8 0.7 copy-start.6
Sparse Core Ops, SparseCore 0:
  9.7 66.0 all-reduce.1
  80.0 210.0 reduce-scatter.1
  293.0 78.6 all-gather.5
  387.5 51.1 all-gather.3

commit v2 on v1

v2 whole, which is shorter than its diff:
```python
import functools

import jax
import jax.numpy as jnp
from jax import lax
from jax.experimental import pallas as pl
from jax.experimental.pallas import tpu as pltpu
from jax.sharding import PartitionSpec as P

GROUP = 16
CHUNK = 128
NY, NZ, NX, NC = 4, 8, 4, 2
f32 = jnp.float32
bf16 = jnp.bfloat16
MESH = pl.DeviceIdType.MESH


def split(value):
    high = value.astype(bf16)
    return high, (value - high.astype(f32)).astype(bf16)


def dot(a, b):
    return jnp.dot(a, b, preferred_element_type=f32)


def dot_three(a, b):
    a_high, a_low = split(a)
    b_high, b_low = split(b)
    return dot(a_high, b_high) + dot(a_low, b_high) + dot(a_high, b_low)


def dot_nt(a, b):
    return lax.dot_general(a, b, (((1,), (1,)), ((), ())), preferred_element_type=f32)


def aligned(index, size):
    return pl.multiple_of(index * size, size)


def kernel(
    tokens_ref,
    gain_ref,
    cols_ref,
    rate_row_ref,
    modes_ref,
    wt_ref,
    emb_ref,
    ow_ref,
    out_ref,
    before,
    ebuf,
    enorm,
    wbuf,
    squares,
    partial,
    partial16,
    arrived,
    table,
    one_hot,
    proj,
    driving,
    conv,
    queries,
    toep_high,
    toep_low,
    to_end,
    from_end,
    zstate,
    ystate,
    ends,
    gated_t,
    gated,
    wo,
    total,
    send_sems,
    recv_sems,
):
    i = lax.axis_index("ctx")
    j = lax.axis_index("fsdp")
    y, z = i // NZ, i % NZ
    x, c = j // NC, j % NC
    up, down = (y + 1) % NY, (y + NY - 1) % NY
    opposite = (y + 2) % NY
    right, left = (x + 1) % NX, (x + NX - 1) % NX
    across = (x + 2) % NX
    share = NY * NZ // (NX * NC)

    def at(yy=None, zz=None, xx=None, cc=None):
        yy = y if yy is None else yy
        zz = z if zz is None else zz
        xx = x if xx is None else xx
        cc = c if cc is None else cc
        return (yy * NZ + zz, xx * NC + cc)

    labels = {}
    sent = []

    def slot(name):
        return labels.setdefault(name, len(labels))

    def send(name, source, target, device):
        k = slot(name)
        copy = pltpu.make_async_remote_copy(
            src_ref=source,
            dst_ref=target,
            send_sem=send_sems.at[k],
            recv_sem=recv_sems.at[k],
            device_id=device,
            device_id_type=MESH,
        )
        copy.start()
        sent.append(copy)
        return copy

    def receive(name, target):
        pltpu.make_async_copy(target, target, recv_sems.at[slot(name)]).wait()

    barrier = pltpu.get_barrier_semaphore()

    def greet(device):
        pl.semaphore_signal(barrier, inc=1, device_id=device, device_id_type=MESH)

    for d in range(1, NZ):
        greet(at(zz=(z + d) % NZ))
    for d in range(1, NY):
        greet(at(yy=(y + d) % NY))
    for d in range(1, NX * NC):
        other = (j + d) % (NX * NC)
        greet((i, other))
    count_ctx = NY * NZ
    greet(((i + 1) % count_ctx, j))
    greet(((i + count_ctx - 1) % count_ctx, j))
    swap_to = (share * j + i % share, i // share)
    swap_from = (share * j + i % share, i // share)
    moves = jnp.logical_or(swap_to[0] != i, swap_to[1] != j)

    @pl.when(moves)
    def _():
        greet(swap_to)

    partners = NZ - 1 + NY - 1 + NX * NC - 1 + 2
    pl.semaphore_wait(barrier, partners + jnp.where(moves, 1, 0))

    parts = (("kv", 256, 512), ("q", 0, 256))
    own_cols = pl.ds(aligned(y, 128), 128)
    for name, first, rows in parts[:1]:
        block = wt_ref.at[pl.ds(first, rows), :]
        target = wbuf.at[pl.ds(first, rows), own_cols]
        send("w_up_" + name, block, target, at(yy=up))
        send("w_down_" + name, block, target, at(yy=down))
    emb_piece = emb_ref.at[pl.ds(aligned(y, 128), 128), pl.ds(aligned(z % share, 128), 128)]
    holder = z // share
    e_slots = [slot("e" + str(k)) for k in range(NX)]
    e_sends = [slot("es" + str(k)) for k in range(NX * NC)]

    def emb_copies():
        copies = []
        for d in range(1, NX * NC):
            other = (j + d) % (NX * NC)
            copies.append(
                pltpu.make_async_remote_copy(
                    src_ref=emb_piece,
                    dst_ref=ebuf.at[x],
                    send_sem=send_sems.at[e_sends[d]],
                    recv_sem=recv_sems.at[e_slots[0] + x],
                    device_id=(i, other),
                    device_id_type=MESH,
                )
            )
        return copies

    @pl.when(c == holder)
    def _():
        for copy in emb_copies():
            copy.start()
        pltpu.make_async_copy(emb_piece, ebuf.at[x], recv_sems.at[e_slots[0] + x]).start()

    for name, first, rows in parts[1:]:
        block = wt_ref.at[pl.ds(first, rows), :]
        target = wbuf.at[pl.ds(first, rows), own_cols]
        send("w_up_" + name, block, target, at(yy=up))
        send("w_down_" + name, block, target, at(yy=down))
    send("tokens", tokens_ref.at[:, pl.ds(384, 128)], before, ((i + 1) % count_ctx, j))

    wo_rows = pl.ds(aligned(2 * y + z // share, 256), 256)
    wo_cols = pl.ds(aligned(z % share, 128), 128)
    swap_rows = pl.ds(aligned(j, 256), 256)
    swap_slot = slot("swap")

    def swap_copy():
        return pltpu.make_async_remote_copy(
            src_ref=ow_ref,
            dst_ref=wo.at[swap_rows, wo_cols],
            send_sem=send_sems.at[swap_slot],
            recv_sem=recv_sems.at[swap_slot],
            device_id=swap_to,
            device_id_type=MESH,
        )

    @pl.when(moves)
    def _():
        swap_copy().start()

    @pl.when(jnp.logical_not(moves))
    def _():
        pltpu.make_async_copy(ow_ref, wo.at[wo_rows, wo_cols], recv_sems.at[swap_slot]).start()

    wbuf[:, own_cols] = wt_ref[...]

    lane = lax.broadcasted_iota(jnp.int32, (CHUNK, CHUNK), 1)
    row = lax.broadcasted_iota(jnp.int32, (CHUNK, CHUNK), 0)
    lane_f = lane.astype(f32)
    row_f = row.astype(f32)
    filters = jnp.zeros((GROUP, CHUNK), f32)
    grid = lax.broadcasted_iota(jnp.int32, (GROUP, CHUNK), 1).astype(f32)
    for m in range(16):
        rate = modes_ref[0, :, m : m + 1]
        filters = filters + modes_ref[1, :, m : m + 1] * jnp.exp(-rate * grid)
    for g in range(16):
        wide = jnp.broadcast_to(filters[g : g + 1, :], (CHUNK, CHUNK))
        rolled = pltpu.roll(wide, 0, 1, stride=1, stride_axis=0)
        high, low = split(jnp.where(lane >= row, rolled, 0.0))
        toep_high[g] = high
        toep_low[g] = low
    for h in range(2):
        to_end[h] = jnp.exp(-rate_row_ref[h : h + 1, :] * (CHUNK - 1 - row_f))
        rate_col = cols_ref[h * 128 : (h + 1) * 128, 1:2]
        res_col = cols_ref[h * 128 : (h + 1) * 128, 2:3]
        from_end[h] = res_col * jnp.exp(-rate_col * (lane_f + 1.0))

    def relay(tag, buffer, name, first, rows):
        half = rows // 2
        from_down = buffer.at[pl.ds(first, rows), pl.ds(aligned(down, 128), 128)]
        receive(tag + "_up_" + name, from_down)
        block = buffer.at[pl.ds(first, half), pl.ds(aligned(down, 128), 128)]
        send(tag + "_on_up_" + name, block, block, at(yy=up))
        from_up = buffer.at[pl.ds(first, rows), pl.ds(aligned(up, 128), 128)]
        receive(tag + "_down_" + name, from_up)
        block = buffer.at[pl.ds(first + half, half), pl.ds(aligned(up, 128), 128)]
        send(tag + "_on_down_" + name, block, block, at(yy=down))

    def relayed(tag, buffer, name, first, rows):
        half = rows // 2
        columns = pl.ds(aligned(opposite, 128), 128)
        receive(tag + "_on_up_" + name, buffer.at[pl.ds(first, half), columns])
        receive(tag + "_on_down_" + name, buffer.at[pl.ds(first + half, half), columns])

    relay("w", wbuf, *parts[0])

    for k in range(NX):
        pltpu.make_async_copy(ebuf.at[k], ebuf.at[k], recv_sems.at[e_slots[k]]).wait()
    ones = jnp.ones((8, 128), bf16)
    square_sum = jnp.zeros((8, 128), f32)
    for k in range(NX):
        piece = ebuf[k].astype(f32)
        high, low = split(piece * piece)
        square_sum = square_sum + dot_nt(ones, high) + dot_nt(ones, low)
        gain = gain_ref[pl.ds(k * NZ + z, 1), :]
        enorm[:, k * 128 : (k + 1) * 128] = (piece * gain).astype(bf16)
    squares[z] = square_sum
    for d in range(1, NZ):
        send("sq" + str(d), squares.at[z], squares.at[z], at(zz=(z + d) % NZ))

    def table_part(name, first, rows):
        piece = rows // NZ
        value = dot_nt(wbuf[first : first + rows, :], enorm[...])
        partial[first : first + rows, :] = value
        partial16[first : first + rows, :] = value.astype(bf16)
        for d in range(1, NZ):
            to = (z + d) % NZ
            source = partial16.at[pl.ds(first + aligned(to, piece), piece), :]
            target = arrived.at[z, pl.ds(first // NZ, piece), :]
            send("rs_" + name + str(d), source, target, at(zz=to))

    relayed("w", wbuf, *parts[0])
    table_part(*parts[0])
    relay("w", wbuf, *parts[1])

    receive("tokens", before)
    earlier = jnp.where(i > 0, before[...], -1)
    vocab_row = lax.broadcasted_iota(jnp.int32, (512, 128), 0)
    one_hot[:, 0:128] = jnp.where(vocab_row == earlier, 1.0, 0.0).astype(bf16)
    for k in range(4):
        these = tokens_ref[:, k * 128 : (k + 1) * 128]
        one_hot[:, (k + 1) * 128 : (k + 2) * 128] = jnp.where(vocab_row == these, 1.0, 0.0).astype(bf16)

    relayed("w", wbuf, *parts[1])
    table_part(*parts[1])

    for d in range(1, NZ):
        receive("sq" + str(d), squares.at[(z + NZ - d) % NZ])
    all_squares = squares[0]
    for k in range(1, NZ):
        all_squares = all_squares + squares[k]
    width = gain_ref.shape[0] * gain_ref.shape[1]
    scale = lax.rsqrt(all_squares * (1.0 / width) + 1e-05)[0:1, :]

    def reduce_part(name, first, rows):
        piece = rows // NZ
        mine = pl.ds(first + aligned(z, piece), piece)
        value = partial[mine, :]
        for d in range(1, NZ):
            origin = (z + NZ - d) % NZ
            receive("rs_" + name + str(d), arrived.at[origin, pl.ds(first // NZ, piece), :])
            value = value + arrived[origin, first // NZ : first // NZ + piece, :].astype(f32)
        table[mine, own_cols] = (value * scale).astype(bf16)
        block = table.at[mine, own_cols]
        for d in range(1, NZ):
            send("ag_" + name + str(d), block, block, at(zz=(z + d) % NZ))

    def spread_part(name, first, rows):
        piece = rows // NZ
        for d in range(1, NZ):
            origin = (z + NZ - d) % NZ
            receive("ag_" + name + str(d), table.at[pl.ds(first + aligned(origin, piece), piece), own_cols])
        block = table.at[pl.ds(first, rows), own_cols]
        send("t_up_" + name, block, block, at(yy=up))
        send("t_down_" + name, block, block, at(yy=down))

    reduce_part(*parts[0])
    reduce_part(*parts[1])
    spread_part(*parts[0])
    spread_part(*parts[1])

    pltpu.make_async_copy(wo.at[wo_rows, wo_cols], wo.at[wo_rows, wo_cols], recv_sems.at[swap_slot]).wait()
    for d in range(1, NZ):
        block = wo.at[wo_rows, wo_cols]
        send("wz" + str(d), block, block, at(zz=(z + d) % NZ))

    relay("t", table, *parts[0])
    relay("t", table, *parts[1])
    relayed("t", table, *parts[0])

    def short_conv(base, g, part):
        value = proj[pl.ds(base + aligned(g, 16), 16), :]
        taps = cols_ref[pl.ds(aligned(g, 16), 16), :]
        result = taps[:, 3 + 7 * part : 4 + 7 * part] * value[:, 128:]
        for lag in range(1, 7):
            k = 3 + 7 * part + lag
            result = result + taps[:, k : k + 1] * pltpu.roll(value, lag, 1)[:, 128:]
        return result

    proj[256:768, :] = dot(table[256:768, :], one_hot[...])

    def drive(g, carry):
        value = short_conv(256, g, 1) * short_conv(512, g, 2)
        for k in range(4):
            driving[g, k] = value[:, k * 128 : (k + 1) * 128]
        return carry

    lax.fori_loop(0, 16, drive, 0)

    own_lanes = lax.broadcasted_iota(jnp.int32, (8, 64, 128), 2) // 16 == lax.broadcasted_iota(
        jnp.int32, (8, 64, 128), 0
    )
    for h in range(2):
        blocks = driving[h * 8 : (h + 1) * 8].reshape(512, 128)
        value = dot_three(blocks, to_end[h]).reshape(8, 64, 128)
        value = jnp.sum(jnp.where(own_lanes, value, 0.0), axis=0)
        ends[h] = value.reshape(4, 16, 128)
        over = jnp.exp(-float(CHUNK) * rate_row_ref[h : h + 1, :])
        state = ends[h, 0]
        for k in range(1, 4):
            state = over * state + ends[h, k]
        zstate[z, h * 16 : (h + 1) * 16, :] = state
    for d in range(1, NZ):
        send("sz" + str(d), zstate.at[z], zstate.at[z], at(zz=(z + d) % NZ))

    relayed("t", table, *parts[1])
    proj[0:256, :] = dot(table[0:256, :], one_hot[...])

    def ask(g, carry):
        queries[pl.ds(aligned(g, 16), 16), :] = short_conv(0, g, 0)
        return carry

    lax.fori_loop(0, 16, ask, 0)

    def inside(g, carry):
        high, low = split(driving[g].reshape(64, 128))
        conv[g] = dot(high, toep_high[g]) + dot(low, toep_high[g]) + dot(high, toep_low[g])
        return carry

    lax.fori_loop(0, 16, inside, 0)

    block_rate = -512.0

    def power(h, steps):
        weight = jnp.exp(rate_row_ref[h : h + 1, :] * (block_rate * jnp.maximum(steps, 0).astype(f32)))
        return jnp.where(steps >= 0, weight, 0.0)

    for d in range(1, NZ):
        receive("sz" + str(d), zstate.at[(z + NZ - d) % NZ])
    for h in range(2):
        part = slice(h * 16, (h + 1) * 16)
        line = jnp.zeros((16, 128), f32)
        for k in range(NZ):
            line = line + power(h, jnp.int32(NZ - 1 - k)) * zstate[k, part, :]
        ystate[y, part, :] = line
    for d in range(1, NY):
        send("sy" + str(d), ystate.at[y], ystate.at[y], at(yy=(y + d) % NY))

    for d in range(1, NZ):
        origin = (z + NZ - d) % NZ
        receive(
            "wz" + str(d),
            wo.at[
                pl.ds(aligned(2 * y + origin // share, 256), 256),
                pl.ds(aligned(origin % share, 128), 128),
            ],
        )
    wo_line = wo.at[pl.ds(aligned(y, 512), 512), :]
    send("wy_up", wo_line, wo_line, at(yy=up))
    send("wy_down", wo_line, wo_line, at(yy=down))

    starts = []
    for h in range(2):
        part = slice(h * 16, (h + 1) * 16)
        start = jnp.zeros((16, 128), f32)
        for k in range(NZ):
            start = start + power(h, z - 1 - k) * zstate[k, part, :]
        starts.append(start)
    for d in range(1, NY):
        receive("sy" + str(d), ystate.at[(y + NY - d) % NY])
    for h in range(2):
        part = slice(h * 16, (h + 1) * 16)
        start = starts[h]
        for k in range(NY):
            steps = jnp.where(k < y, z + NZ * (y - 1 - k), -1)
            start = start + power(h, steps) * ystate[k, part, :]
        over = jnp.exp(-float(CHUNK) * rate_row_ref[h : h + 1, :])
        states = [start]
        for k in range(3):
            states.append(over * states[-1] + ends[h, k])
        state = jnp.concatenate(states, axis=0)
        wide = jnp.where(own_lanes, jnp.broadcast_to(state[None], (8, 64, 128)), 0.0)
        value = dot_three(wide.reshape(512, 128), from_end[h]).reshape(8, 64, 128)
        conv[h * 8 : (h + 1) * 8] = conv[h * 8 : (h + 1) * 8] + value

    def gate(g, carry):
        here = pl.ds(aligned(g, 16), 16)
        skip = cols_ref[here, 0:1]
        for k in range(4):
            response = conv[g, k * 16 : (k + 1) * 16, :] + skip * driving[g, k]
            gated_t[here, k * 128 : (k + 1) * 128] = queries[here, k * 128 : (k + 1) * 128] * response
        return carry

    lax.fori_loop(0, 16, gate, 0)
    for k in range(4):
        for h in range(2):
            block = gated_t[h * 128 : (h + 1) * 128, k * 128 : (k + 1) * 128]
            gated[j, k * 128 : (k + 1) * 128, h * 128 : (h + 1) * 128] = block.T.astype(bf16)

    halves = (pl.ds(0, 256), pl.ds(256, 256))
    own = [gated.at[j, half, :] for half in halves]
    send("g_right0", own[0], own[0], at(xx=right))
    send("g_left1", own[1], own[1], at(xx=left))
    send("g_right1", own[1], own[1], at(xx=right))
    send("g_left0", own[0], own[0], at(xx=left))
    send("g_mate", gated.at[j], gated.at[j], at(cc=1 - c))

    wo_down = pl.ds(aligned(down, 512), 512)
    wo_up = pl.ds(aligned(up, 512), 512)
    receive("wy_up", wo.at[wo_down, :])
    block = wo.at[pl.ds(aligned(2 * down, 256), 256), :]
    send("wy_on_up", block, block, at(yy=up))
    receive("wy_down", wo.at[wo_up, :])
    block = wo.at[pl.ds(aligned(2 * up + 1, 256), 256), :]
    send("wy_on_down", block, block, at(yy=down))

    left_j, right_j, across_j = left * NC + c, right * NC + c, across * NC + c
    from_left = [gated.at[left_j, half, :] for half in halves]
    from_right = [gated.at[right_j, half, :] for half in halves]
    from_across = [gated.at[across_j, half, :] for half in halves]
    mate = at(cc=1 - c)
    receive("g_right0", from_left[0])
    send("g_on_right", from_left[0], from_left[0], at(xx=right))
    receive("g_left1", from_right[1])
    send("g_on_left", from_right[1], from_right[1], at(xx=left))
    send("m_left0", from_left[0], from_left[0], mate)
    send("m_right1", from_right[1], from_right[1], mate)
    receive("g_right1", from_left[1])
    send("m_left1", from_left[1], from_left[1], mate)
    receive("g_left0", from_right[0])
    send("m_right0", from_right[0], from_right[0], mate)

    receive("wy_on_up", wo.at[pl.ds(aligned(2 * opposite, 256), 256), :])
    receive("wy_on_down", wo.at[pl.ds(aligned(2 * opposite + 1, 256), 256), :])

    def product(index):
        return dot(gated[index], wo[pl.ds(aligned(index, 256), 256), :])

    mate_j = x * NC + 1 - c
    total[...] = product(j)
    receive("g_mate", gated.at[mate_j])
    total[...] += product(mate_j)
    total[...] += product(left_j)
    total[...] += product(right_j)
    receive("g_on_right", from_across[0])
    send("m_across0", from_across[0], from_across[0], mate)
    receive("g_on_left", from_across[1])
    send("m_across1", from_across[1], from_across[1], mate)
    for name, place in (("left", left), ("right", right), ("across", across)):
        index = place * NC + 1 - c
        if name == "across":
            total[...] += product(across_j)
        receive("m_" + name + "0", gated.at[index, halves[0], :])
        receive("m_" + name + "1", gated.at[index, halves[1], :])
        if name == "across":
            out_ref[...] = (total[...] + product(index)).astype(bf16)
        else:
            total[...] += product(index)

    for copy in sent:
        copy.wait_send()

    @pl.when(c == holder)
    def _():
        for copy in emb_copies():
            copy.wait_send()

    @pl.when(moves)
    def _():
        swap_copy().wait_send()


SEMAPHORES = 112


def body(
    tokens,
    embedding,
    norm_gain,
    in_weight,
    short_taps,
    decay_rates,
    residue,
    skip_weight,
    out_weight,
):
    rates = decay_rates.T
    residues = residue.T
    cols = jnp.concatenate(
        [
            skip_weight[:, None],
            rates.reshape(256, 1),
            residues.reshape(256, 1),
            short_taps.transpose(2, 1, 0).reshape(256, 21),
        ],
        axis=1,
    )
    wt = in_weight.transpose(1, 2, 0).reshape(768, 128)
    whole = pl.BlockSpec(memory_space=pltpu.VMEM)
    outside = pl.BlockSpec(memory_space=pl.ANY)
    vm = pltpu.VMEM
    return pl.pallas_call(
        kernel,
        out_shape=jax.ShapeDtypeStruct((512, 512), bf16),
        in_specs=[whole] * 6 + [outside] * 2,
        out_specs=whole,
        scratch_shapes=[
            vm((1, 128), jnp.int32),
            vm((NX, 128, 128), bf16),
            vm((128, 512), bf16),
            vm((768, 512), bf16),
            vm((NZ, 8, 128), f32),
            vm((768, 128), f32),
            vm((768, 128), bf16),
            vm((NZ, 96, 128), bf16),
            vm((768, 512), bf16),
            vm((512, 640), bf16),
            vm((768, 640), f32),
            vm((16, 4, 16, 128), f32),
            vm((16, 64, 128), f32),
            vm((256, 512), f32),
            vm((16, 128, 128), bf16),
            vm((16, 128, 128), bf16),
            vm((2, 128, 128), f32),
            vm((2, 128, 128), f32),
            vm((NZ, 32, 128), f32),
            vm((NY, 32, 128), f32),
            vm((2, 4, 16, 128), f32),
            vm((256, 512), f32),
            vm((NX * NC, 512, 256), bf16),
            vm((2048, 512), bf16),
            vm((512, 512), f32),
            pltpu.SemaphoreType.DMA((SEMAPHORES,)),
            pltpu.SemaphoreType.DMA((SEMAPHORES,)),
        ],
        compiler_params=pltpu.CompilerParams(
            collective_id=0, has_side_effects=True, vmem_limit_bytes=48 * 1024 * 1024
        ),
    )(
        tokens.reshape(1, 512),
        norm_gain.reshape(32, 128),
        cols,
        rates.reshape(2, 128),
        jnp.stack([rates, residues]),
        wt,
        embedding,
        out_weight,
    )


def solution(mesh):
    placed = (
        P("ctx"),
        P(None, "fsdp"),
        P(),
        P("ctx", None, "fsdp"),
        P(None, None, "fsdp"),
        P(None, "fsdp"),
        P(None, "fsdp"),
        P("fsdp"),
        P("fsdp", "ctx"),
    )
    return jax.shard_map(
        body, mesh=mesh, in_specs=placed, out_specs=P("ctx", "fsdp"), check_vma=False
    )
```

time: 450 us -> 82.6 us (0.18)
  the two profiles are of different devices: /device:TPU:1 before, /device:TPU:13 now
where the time goes in v2:
time: 82.6 us; the launch traced here: 82.4 us
  Pallas kernels  77.1 us (93%)
  local copies, waits for them, and re-layouts  4.55 us (6%)
    pallas_call x1, Pallas kernels, body(): pl.pallas_call(kernel, out_shape=jax.ShapeDtypeStruct((512, 512), bf16),...  77.1 us
    unnamed x13, local copies, waits for them, and re-layouts  2.35 us

profile of v2, /device:TPU:13, one launch (start us, length us, event | category | flops | bytes accessed | tf_op | source)
XLA Modules:
  0.0 82.4 jit_solution(3802646490360251024)
XLA Ops:
  0.0 0.0 copy-start.4
  0.0 0.0 copy-start
  0.0 0.7 copy-done.4
  0.7 0.1 copy.23
  0.8 0.1 reshape.26.rate_row_ref
  0.9 0.1 reshape.23
  0.9 0.8 copy.24
  1.7 0.1 reshape.24
  1.8 0.7 reshape.25
  2.5 0.7 pad_maximum_fusion
  3.2 0.1 copy.26.cols_ref
  3.3 0.0 copy-start.1
  3.3 0.0 copy-start.2
  3.3 0.0 copy-start.3
  3.4 1.1 %copy.25 = bf16[3,256,128]{2,1,0:T(8,128)(2,1)S(1)} copy(bf16[3,256,128]{1,2,0:T(8,128)(2,1)} %bitcast.17) | data formatting | bytes 393216 | tf_op jit(solution)/shard_map/transpose | solution.py:552
  4.5 0.0 copy-done
  4.5 0.0 copy-done.1
  4.5 0.0 copy-done.2
  4.5 0.0 copy-done.3
  4.5 77.1 %shard_map.91 = bf16[512,512]{1,0:T(8,128)(2,1)S(1)} custom-call(s32[1,512]{1,0:T(1,128)S(1)} %bitcast.16, f32[32,128]{1,0:T(8,128)S(1)} %bitcast.15, f32[256,24]{1,0:T(8,128)S(1)} %copy.26.cols_ref, f32[2,128]{1,0:T(2,128)S(1)} %reshape.26.rate_row_ref, f32[2,16,16]{2,1,0:T(8,128)S(1)} %pad_maximum_fusion.1.modes_ref, bf16[768,128]{1,0:T(8,128)(2,1)S(1)} %bitcast.14, ...), custom_call_target="tpu_custom_call" | custom-call | tf_op jit(solution)/shard_map/pallas_call | solution.py:556
  81.6 0.8 copy.28
  (1 shorter events, 0.0 us)
Async XLA Ops:
  0.0 0.7 copy-start.4
  0.0 4.5 %copy-start = (bf16[512,512]{1,0:T(8,128)(2,1)S(1)}, bf16[512,512]{1,0:T(8,128)(2,1)}, u32[]{:S(2)}) copy-start(bf16[512,512]{1,0:T(8,128)(2,1)} %emb_ref.1) | copy-start | bytes 1572868
  3.3 1.2 %copy-start.1 = (bf16[256,128]{1,0:T(8,128)(2,1)S(1)}, bf16[256,128]{1,0:T(8,128)(2,1)}, u32[]{:S(2)}) copy-start(bf16[256,128]{1,0:T(8,128)(2,1)} %ow_ref.1) | copy-start | bytes 196612
  3.3 1.2 %copy-start.2 = (f32[4096]{0:T(1024)S(1)}, f32[4096]{0:T(1024)}, u32[]{:S(2)}) copy-start(f32[4096]{0:T(1024)} %param.11) | copy-start | bytes 49156
  3.3 1.2 %copy-start.3 = (s32[512]{0:T(512)S(1)}, s32[512]{0:T(512)}, u32[]{:S(2)}) copy-start(s32[512]{0:T(512)} %param.9) | copy-start | bytes 6148

commit v3 on v1

v3 whole, which is shorter than its diff:
```python
import functools

import jax
import jax.numpy as jnp
from jax import lax
from jax.experimental import pallas as pl
from jax.experimental.pallas import tpu as pltpu
from jax.sharding import PartitionSpec as P

GROUP = 16
CHUNK = 128
NY, NZ, NX, NC = 4, 8, 4, 2
f32 = jnp.float32
bf16 = jnp.bfloat16
MESH = pl.DeviceIdType.MESH


def split(value):
    high = value.astype(bf16)
    return high, (value - high.astype(f32)).astype(bf16)


def dot(a, b):
    return jnp.dot(a, b, preferred_element_type=f32)


def dot_three(a, b):
    a_high, a_low = split(a)
    b_high, b_low = split(b)
    return dot(a_high, b_high) + dot(a_low, b_high) + dot(a_high, b_low)


def dot_nt(a, b):
    return lax.dot_general(a, b, (((1,), (1,)), ((), ())), preferred_element_type=f32)


def aligned(index, size):
    return pl.multiple_of(index * size, size)


def kernel(
    tokens_ref,
    gain_ref,
    skip_ref,
    taps_ref,
    rates_ref,
    residue_ref,
    w_ref,
    emb_ref,
    ow_ref,
    out_ref,
    wt,
    wbuf,
    ebuf,
    enorm,
    squares,
    send_kv,
    send_q,
    arrived_kv,
    arrived_q,
    own_kv,
    own_q,
    table,
    tokens,
    token_mat,
    one_hot,
    short_in,
    taps,
    driving,
    queries,
    convolved,
    gated_f,
    gated_b,
    landed,
    gated,
    wo,
    total,
    send_sems,
    recv_sems,
):
    i = lax.axis_index("ctx")
    j = lax.axis_index("fsdp")
    y, z = i // NZ, i % NZ
    x, c = j // NC, j % NC
    up, down = (y + 1) % NY, (y + NY - 1) % NY
    opposite = (y + 2) % NY
    right, left = (x + 1) % NX, (x + NX - 1) % NX
    across = (x + 2) % NX
    count_ctx = NY * NZ
    count_fsdp = NX * NC
    share = count_ctx // count_fsdp

    def at(yy=None, zz=None, xx=None, cc=None):
        yy = y if yy is None else yy
        zz = z if zz is None else zz
        xx = x if xx is None else xx
        cc = c if cc is None else cc
        return (yy * NZ + zz, xx * NC + cc)

    labels = {}
    sent = []

    def slot(name):
        return labels.setdefault(name, len(labels))

    def remote(name, source, target, device):
        k = slot(name)
        return pltpu.make_async_remote_copy(
            src_ref=source,
            dst_ref=target,
            send_sem=send_sems.at[k],
            recv_sem=recv_sems.at[k],
            device_id=device,
            device_id_type=MESH,
        )

    def send(name, source, target, device):
        copy = remote(name, source, target, device)
        copy.start()
        sent.append(copy)

    def receive(name, target):
        pltpu.make_async_copy(target, target, recv_sems.at[slot(name)]).wait()

    barrier = pltpu.get_barrier_semaphore()

    def greet(device):
        pl.semaphore_signal(barrier, inc=1, device_id=device, device_id_type=MESH)

    for d in range(1, count_ctx):
        greet(((i + d) % count_ctx, j))
    for d in range(1, count_fsdp):
        greet((i, (j + d) % count_fsdp))
    swap_to = (share * j + i % share, i // share)
    moves = jnp.logical_or(swap_to[0] != i, swap_to[1] != j)

    @pl.when(moves)
    def _():
        greet(swap_to)

    for group in range(3):
        for h in range(2):
            block = w_ref[group, :, h * 128 : (h + 1) * 128].astype(f32)
            wt[group, h * 128 : (h + 1) * 128, :] = block.T.astype(bf16)
    ones = jnp.ones((8, 512), bf16)
    piece = emb_ref[...].astype(f32)
    high, low = split(piece * piece)
    squares[j] = (dot_nt(ones, high) + dot_nt(ones, low))[0:1, :]

    pl.semaphore_wait(barrier, count_ctx - 1 + count_fsdp - 1 + jnp.where(moves, 1, 0))

    holder = z // share
    e_slots = [slot("e" + str(k)) for k in range(NX)]
    emb_piece = emb_ref.at[:, pl.ds(aligned(z % share, 128), 128)]

    def emb_copy(k, source, place, device):
        return pltpu.make_async_remote_copy(
            src_ref=source,
            dst_ref=ebuf.at[place],
            send_sem=send_sems.at[slot("es" + str(k))],
            recv_sem=recv_sems.at[e_slots[0] + place],
            device_id=device,
            device_id_type=MESH,
        )

    mate = at(cc=1 - c)

    def emb_copies():
        copies = [emb_copy(d, emb_piece, x, at(xx=(x + d) % NX)) for d in (2, 1, 3)]
        return copies + [emb_copy(0, emb_piece, x, mate)]

    def emb_relays():
        places = [(x + d) % NX for d in (1, 3, 2)]
        return [(place, emb_copy(4 + n, ebuf.at[place], place, mate)) for n, place in enumerate(places)]

    @pl.when(c == holder)
    def _():
        for copy in emb_copies():
            copy.start()
        pltpu.make_async_copy(emb_piece, ebuf.at[x], recv_sems.at[e_slots[0] + x]).start()

    def w_rows(to):
        return wt.at[:, pl.ds(aligned(to, 64), 64), :]

    for d in (2, 1, 3):
        to = (y + d) % NY
        send("w" + str(d), w_rows(to), wbuf.at[y], at(yy=to))

    for d in range(1, NZ):
        send("tz" + str(d), tokens_ref, tokens.at[y, z], at(zz=(z + d) % NZ))
    for d in range(1, count_fsdp):
        send("sq" + str(d), squares.at[j], squares.at[j], (i, (j + d) % count_fsdp))

    wo_rows = pl.ds(aligned(2 * y + z // share, 256), 256)
    wo_cols = pl.ds(aligned(z % share, 128), 128)
    wo_own = wo.at[wo_rows, wo_cols]

    def swap_copy():
        return remote("swap", ow_ref, wo.at[pl.ds(aligned(j, 256), 256), wo_cols], swap_to)

    @pl.when(moves)
    def _():
        swap_copy().start()

    @pl.when(jnp.logical_not(moves))
    def _():
        pltpu.make_async_copy(ow_ref, wo_own, recv_sems.at[slot("swap")]).start()

    wbuf[y] = wt[:, pl.ds(aligned(y, 64), 64), :]
    tokens[y, z] = tokens_ref[...]

    row = lax.broadcasted_iota(jnp.int32, (CHUNK, CHUNK), 0)
    lane = lax.broadcasted_iota(jnp.int32, (CHUNK, CHUNK), 1)
    group_lane = lax.broadcasted_iota(jnp.int32, (16, 16), 1) == i // 2
    rate = jnp.sum(jnp.where(group_lane, rates_ref[...], 0.0), axis=1, keepdims=True)
    weight = jnp.sum(jnp.where(group_lane, residue_ref[...], 0.0), axis=1, keepdims=True)
    steps = lax.broadcasted_iota(jnp.int32, (16, CHUNK), 1).astype(f32)
    rate = jnp.broadcast_to(rate, (16, CHUNK))
    weight = jnp.broadcast_to(weight, (16, CHUNK))
    filters = jnp.sum(weight * jnp.exp(-rate * steps), axis=0, keepdims=True)
    rolled = pltpu.roll(jnp.broadcast_to(filters, (CHUNK, CHUNK)), 0, 1, stride=1, stride_axis=0)
    toeplitz = jnp.where(lane >= row, rolled, 0.0).T
    to_end = jnp.exp(-rate * (CHUNK - 1 - steps))
    from_start = weight * jnp.exp(-rate * (steps + 1.0))
    from_start = jnp.concatenate([from_start, jnp.zeros((CHUNK - 16, CHUNK), f32)], axis=0).T

    pick = lax.broadcasted_iota(jnp.int32, (8, 256), 1) == 8 * i + lax.broadcasted_iota(jnp.int32, (8, 256), 0)
    skips = jnp.sum(jnp.where(pick, skip_ref[...], 0.0), axis=1, keepdims=True)
    skips = jnp.broadcast_to(skips, (8, CHUNK))
    for group in range(3):
        for lag in range(7):
            value = jnp.where(pick, taps_ref[group, lag : lag + 1, :], 0.0)
            taps[group, lag] = jnp.broadcast_to(jnp.sum(value, axis=1, keepdims=True), (8, CHUNK))

    @pl.when(c == holder)
    def _():
        pltpu.make_async_copy(ebuf.at[x], ebuf.at[x], recv_sems.at[e_slots[0] + x]).wait()
        for place, copy in emb_relays():
            pltpu.make_async_copy(ebuf.at[place], ebuf.at[place], recv_sems.at[e_slots[0] + place]).wait()
            copy.start()

    @pl.when(c != holder)
    def _():
        for k in range(NX):
            pltpu.make_async_copy(ebuf.at[k], ebuf.at[k], recv_sems.at[e_slots[k]]).wait()

    for k in range(NY):
        gain = gain_ref[pl.ds(k * NZ + z, 1), :]
        enorm[:, k * 128 : (k + 1) * 128] = (ebuf[k].astype(f32) * gain).astype(bf16)
    for d in range(1, NY):
        receive("w" + str(d), wbuf.at[(y + NY - d) % NY])

    def partial(group):
        weights = jnp.concatenate([wbuf[k, group] for k in range(NY)], axis=1)
        return dot_nt(weights, enorm[...])

    keys, values = partial(1), partial(2)
    for k in range(NZ):
        part = slice(k * 8, (k + 1) * 8)
        send_kv[k] = jnp.concatenate([keys[part], values[part]], axis=0).astype(bf16)
    for d in (4, 3, 5, 2, 6, 1, 7):
        to = (z + d) % NZ
        send("kv" + str(d), send_kv.at[to], arrived_kv.at[z], at(zz=to))
    asks = partial(0)
    for k in range(NZ):
        part = slice(k * 8, (k + 1) * 8)
        send_q[k] = jnp.concatenate([asks[part, 0:256], asks[part, 256:512]], axis=0).astype(bf16)
    for d in (4, 3, 5, 2, 6, 1, 7):
        to = (z + d) % NZ
        send("q" + str(d), send_q.at[to], arrived_q.at[z], at(zz=to))
    own_kv[...] = send_kv[z].astype(f32)
    own_q[...] = send_q[z].astype(f32)

    for d in range(1, NZ):
        receive("tz" + str(d), tokens.at[y, (z + NZ - d) % NZ])
    for d in range(1, NY):
        send("ty" + str(d), tokens.at[y], tokens.at[y], at(yy=(y + d) % NY))

    receive("swap", wo_own)
    for d in (2, 6, 1, 7):
        send("wz" + str(d), wo_own, wo_own, at(zz=(z + d) % NZ))

    for d in range(1, NY):
        receive("ty" + str(d), tokens.at[(y + NY - d) % NY])
    for k in range(count_ctx):
        token_mat[k * 4 : (k + 1) * 4, :] = tokens[k // NZ, k % NZ].astype(f32)
    token_mat[...] = token_mat[...].T
    vocab_row = lax.broadcasted_iota(jnp.int32, (512, 128), 0).astype(f32)

    def mark(n, carry):
        for h in range(2):
            these = token_mat[pl.ds(2 * n + h, 1), :]
            hits = jnp.where(vocab_row == these, 1.0, 0.0)
            one_hot[n, :, h * 128 : (h + 1) * 128] = hits.astype(bf16)
        return carry

    lax.fori_loop(0, 64, mark, 0)

    def wo_place(origin, half=None):
        rows, first = (256, 0) if half is None else (128, half * 128)
        return wo.at[
            pl.ds(aligned(2 * y + origin // share, 256) + first, rows),
            pl.ds(aligned(origin % share, 128), 128),
        ]

    for d in range(1, count_fsdp):
        receive("sq" + str(d), squares.at[(j + count_fsdp - d) % count_fsdp])
    all_squares = squares[0]
    for k in range(1, count_fsdp):
        all_squares = all_squares + squares[k]
    width = gain_ref.shape[0] * gain_ref.shape[1]
    scale = lax.rsqrt(all_squares * (1.0 / width) + 1e-05)

    value = own_kv[...]
    for d in (1, 7, 2, 6, 3, 5, 4):
        origin = (z + NZ - d) % NZ
        receive("kv" + str(d), arrived_kv.at[origin])
        value = value + arrived_kv[origin].astype(f32)
    table[8:24, :] = value * scale
    value = own_q[...]
    for d in (1, 7, 2, 6, 3, 5, 4):
        origin = (z + NZ - d) % NZ
        receive("q" + str(d), arrived_q.at[origin])
        value = value + arrived_q[origin].astype(f32)
    table[0:8, :] = jnp.concatenate([value[0:8], value[8:16]], axis=1) * scale
    table[24:32, :] = jnp.zeros((8, 512), f32)

    for d in (1, 7, 2, 6):
        receive("wz" + str(d), wo_place((z + NZ - d) % NZ))
    ahead, behind = at(zz=(z + 2) % NZ), at(zz=(z + NZ - 2) % NZ)
    block = wo_place((z + NZ - 1) % NZ)
    send("wz3", block, block, ahead)
    block = wo_place((z + 1) % NZ)
    send("wz5", block, block, behind)
    block = wo_place((z + NZ - 2) % NZ, 0)
    send("wz4a", block, block, ahead)
    block = wo_place((z + 2) % NZ, 1)
    send("wz4b", block, block, behind)

    table16 = table[...].astype(bf16)

    def look_up(n, carry):
        found = dot(table16, one_hot[n])
        for group in range(3):
            for h in range(2):
                rows = pl.ds(aligned(2 * n + h + 8, 8), 8)
                short_in[group, rows, :] = found[group * 8 : (group + 1) * 8, h * 128 : (h + 1) * 128]
        return carry

    lax.fori_loop(0, 64, look_up, 0, unroll=4)
    for group in range(3):
        tail = short_in[group, 1024:1088, :]
        shifted = pltpu.roll(tail, 1, 1)
        first_lane = lax.broadcasted_iota(jnp.int32, (64, 128), 1) == 0
        short_in[group, 0:64, :] = jnp.where(first_lane, 0.0, shifted)

    def convolve(n, carry):
        sums = []
        for group in range(3):
            result = taps[group, 0] * short_in[group, pl.ds(aligned(n + 8, 8), 8), :]
            for lag in range(1, 7):
                rows = pl.ds(aligned(n + 8 - lag, 8), 8)
                result = result + taps[group, lag] * short_in[group, rows, :]
            sums.append(result)
        here = pl.ds(aligned(n, 8), 8)
        queries[here, :] = sums[0]
        driving[here, :] = sums[1] * sums[2]
        return carry

    lax.fori_loop(0, 128, convolve, 0, unroll=4)

    receive("wz3", wo_place((z + NZ - 3) % NZ))
    receive("wz5", wo_place((z + 3) % NZ))
    receive("wz4a", wo_place((z + 4) % NZ, 0))
    receive("wz4b", wo_place((z + 4) % NZ, 1))
    wo_line = wo.at[pl.ds(aligned(y, 512), 512), :]
    send("wy_up", wo_line, wo_line, at(yy=up))
    send("wy_down", wo_line, wo_line, at(yy=down))

    planes = [driving[pl.ds(k, CHUNK, stride=8), :] for k in range(8)]
    wide = jnp.concatenate(planes, axis=1)
    ends = dot_three(to_end, wide)
    states = jnp.concatenate([ends[:, k * 128 : (k + 1) * 128] for k in range(8)], axis=0)
    rates = jnp.concatenate([rate] * 8, axis=0)

    def later(value, count):
        return jnp.where(lane >= count, pltpu.roll(value, count, 1), 0.0)

    for level in range(7):
        reach = 1 << level
        states = states + jnp.exp(-rates * float(CHUNK * reach)) * later(states, reach)
    states = later(states, 1)
    starts = jnp.concatenate([states[k * 16 : (k + 1) * 16] for k in range(8)], axis=1)
    starts = jnp.concatenate([starts, jnp.zeros((CHUNK - 16, 1024), f32)], axis=0)
    convolved[...] = dot_three(toeplitz, wide) + dot_three(from_start, starts)
    for k in range(8):
        response = convolved[:, k * 128 : (k + 1) * 128] + skips[k : k + 1, :] * planes[k]
        result = queries[pl.ds(k, CHUNK, stride=8), :] * response
        gated_f[pl.ds(k, CHUNK, stride=8), :] = result.T
    gated_b[...] = gated_f[...].astype(bf16)

    def positions(index):
        return gated_b.at[pl.ds(aligned(index, 32), 32), :]

    far = sorted(range(1, count_ctx), key=lambda d: -min(d % NZ, NZ - d % NZ))
    for d in far:
        to = (i + d) % count_ctx
        send("a" + str(d), positions(to), landed.at[i], (to, j))
    landed[i] = gated_b[pl.ds(aligned(i, 32), 32), :]
    for d in reversed(far):
        receive("a" + str(d), landed.at[(i + count_ctx - d) % count_ctx])
    for k in range(4):
        for h in range(2):
            blocks = [landed[n].astype(f32)[k * 8 : (k + 1) * 8] for n in range(h * 16, (h + 1) * 16)]
            block = jnp.concatenate(blocks, axis=0)
            gated[j, k * 128 : (k + 1) * 128, h * 128 : (h + 1) * 128] = block.T.astype(bf16)

    halves = (pl.ds(0, 256), pl.ds(256, 256))
    own = [gated.at[j, half, :] for half in halves]
    send("g_right0", own[0], own[0], at(xx=right))
    send("g_left1", own[1], own[1], at(xx=left))
    send("g_right1", own[1], own[1], at(xx=right))
    send("g_left0", own[0], own[0], at(xx=left))
    send("g_mate", gated.at[j], gated.at[j], at(cc=1 - c))

    wo_down = pl.ds(aligned(down, 512), 512)
    wo_up = pl.ds(aligned(up, 512), 512)
    receive("wy_up", wo.at[wo_down, :])
    block = wo.at[pl.ds(aligned(2 * down, 256), 256), :]
    send("wy_on_up", block, block, at(yy=up))
    receive("wy_down", wo.at[wo_up, :])
    block = wo.at[pl.ds(aligned(2 * up + 1, 256), 256), :]
    send("wy_on_down", block, block, at(yy=down))

    left_j, right_j, across_j = left * NC + c, right * NC + c, across * NC + c
    from_left = [gated.at[left_j, half, :] for half in halves]
    from_right = [gated.at[right_j, half, :] for half in halves]
    from_across = [gated.at[across_j, half, :] for half in halves]
    receive("g_right0", from_left[0])
    send("g_on_right", from_left[0], from_left[0], at(xx=right))
    receive("g_left1", from_right[1])
    send("g_on_left", from_right[1], from_right[1], at(xx=left))
    send("m_left0", from_left[0], from_left[0], mate)
    send("m_right1", from_right[1], from_right[1], mate)
    receive("g_right1", from_left[1])
    send("m_left1", from_left[1], from_left[1], mate)
    receive("g_left0", from_right[0])
    send("m_right0", from_right[0], from_right[0], mate)

    receive("wy_on_up", wo.at[pl.ds(aligned(2 * opposite, 256), 256), :])
    receive("wy_on_down", wo.at[pl.ds(aligned(2 * opposite + 1, 256), 256), :])

    def product(index):
        return dot(gated[index], wo[pl.ds(aligned(index, 256), 256), :])

    mate_j = x * NC + 1 - c
    total[...] = product(j)
    receive("g_mate", gated.at[mate_j])
    total[...] += product(mate_j)
    total[...] += product(left_j)
    total[...] += product(right_j)
    receive("g_on_right", from_across[0])
    send("m_across0", from_across[0], from_across[0], mate)
    receive("g_on_left", from_across[1])
    send("m_across1", from_across[1], from_across[1], mate)
    for name, place in (("left", left), ("right", right), ("across", across)):
        index = place * NC + 1 - c
        if name == "across":
            total[...] += product(across_j)
        receive("m_" + name + "0", gated.at[index, halves[0], :])
        receive("m_" + name + "1", gated.at[index, halves[1], :])
        if name == "across":
            out_ref[...] = (total[...] + product(index)).astype(bf16)
        else:
            total[...] += product(index)

    for copy in sent:
        copy.wait_send()

    @pl.when(c == holder)
    def _():
        for copy in emb_copies():
            copy.wait_send()
        for _, copy in emb_relays():
            copy.wait_send()

    @pl.when(moves)
    def _():
        swap_copy().wait_send()


SEMAPHORES = 160


def body(
    tokens,
    embedding,
    norm_gain,
    in_weight,
    short_taps,
    decay_rates,
    residue,
    skip_weight,
    out_weight,
):
    whole = pl.BlockSpec(memory_space=pltpu.VMEM)
    outside = pl.BlockSpec(memory_space=pl.ANY)
    vm = pltpu.VMEM
    return pl.pallas_call(
        kernel,
        out_shape=jax.ShapeDtypeStruct((512, 512), bf16),
        in_specs=[whole] * 8 + [outside],
        out_specs=whole,
        scratch_shapes=[
            vm((3, 256, 128), bf16),
            vm((NY, 3, 64, 128), bf16),
            vm((NX, 512, 128), bf16),
            vm((512, 512), bf16),
            vm((NX * NC, 1, 512), f32),
            vm((NZ, 16, 512), bf16),
            vm((NZ, 16, 256), bf16),
            vm((NZ, 16, 512), bf16),
            vm((NZ, 16, 256), bf16),
            vm((16, 512), f32),
            vm((16, 256), f32),
            vm((32, 512), f32),
            vm((NY, NZ, 4, 128), jnp.int32),
            vm((128, 128), f32),
            vm((64, 512, 256), bf16),
            vm((3, 1088, 128), f32),
            vm((3, 7, 8, 128), f32),
            vm((1024, 128), f32),
            vm((1024, 128), f32),
            vm((128, 1024), f32),
            vm((1024, 128), f32),
            vm((1024, 128), bf16),
            vm((NY * NZ, 32, 128), bf16),
            vm((NX * NC, 512, 256), bf16),
            vm((2048, 512), bf16),
            vm((512, 512), f32),
            pltpu.SemaphoreType.DMA((SEMAPHORES,)),
            pltpu.SemaphoreType.DMA((SEMAPHORES,)),
        ],
        compiler_params=pltpu.CompilerParams(
            collective_id=0, has_side_effects=True, vmem_limit_bytes=48 * 1024 * 1024
        ),
    )(
        tokens.reshape(4, 128),
        norm_gain.reshape(32, 128),
        skip_weight.reshape(1, 256),
        short_taps.transpose(1, 0, 2),
        decay_rates,
        residue,
        in_weight.transpose(1, 0, 2),
        embedding,
        out_weight,
    )


def solution(mesh):
    placed = (
        P("ctx"),
        P(None, "fsdp"),
        P(),
        P("ctx", None, "fsdp"),
        P(None, None, "fsdp"),
        P(None, "fsdp"),
        P(None, "fsdp"),
        P("fsdp"),
        P("fsdp", "ctx"),
    )
    return jax.shard_map(
        body, mesh=mesh, in_specs=placed, out_specs=P("ctx", "fsdp"), check_vma=False
    )
```

time: 450 us -> 74.9 us (0.17)
  waiting for transfers between devices: 190 us -> 0 us
  blocking collectives: 143 us -> 0 us
  Pallas kernels: 0 us -> 67.3 us
  local copies, waits for them, and re-layouts: 71 us -> 7.13 us
  between operations: 13.4 us -> 0.02 us
  matrix products: 13.2 us -> 0 us
  starting transfers between devices: 12.7 us -> 0 us
  other arithmetic: 6.03 us -> 0 us
    all_gather x2 -> x0, blocking collectives: 83.8 us -> none  [the longest x1 47 us: body(): totals = lax.all_gather(total, 'ctx', axis=0)]
    reduce_scatter x1 -> x0, waiting for transfers between devices: 77.1 us -> none  [body(): lax.psum_scatter(partial_table, 'ctx', scatter_dimension=0, tiled=True)]
    pallas_call x0 -> x1, Pallas kernels: none -> 67.3 us  [body(): pl.pallas_call(kernel, out_shape=jax.ShapeDtypeStruct((512, 512), bf16),...]
    psum x1 -> x0, waiting for transfers between devices: 65.6 us -> none  [body(): piece = lax.psum(piece, 'fsdp').astype(jnp.float32)]
    gather x2 -> x0, local copies, waits for them, and re-layouts: 59.7 us -> none  [body(): toeplitz = jnp.where(lag_grid >= 0, jnp.take(filters, index, axis=1), 0.0)]
    psum x1 -> x0, blocking collectives: 59.5 us -> none  [body(): squares = lax.psum(jnp.sum(piece * piece, axis=1), 'ctx')]
    all_gather x2 -> x0, waiting for transfers between devices: 46 us -> none  [the longest x1 45.9 us: body(): every = lax.all_gather(gated, 'fsdp', axis=1, tiled=True)]
    dot_general x6 -> x0, matrix products: 13.2 us -> none  [the longest x1 4.29 us: body(): jnp.dot(every, out_panel, preferred_element_type=jnp.float32)]
  transfers between devices with their start and end apart: 6 -> 0, of which waited for: 4 -> 0; matrix products, arithmetic and copies ran while one was open for 18% -> 0% of each run, Pallas kernels for 0% -> 0%
where the time goes in v3:
time: 74.9 us; the launch traced here: 74.5 us
  Pallas kernels  67.3 us (90%)
  local copies, waits for them, and re-layouts  7.13 us (10%)
    pallas_call x1, Pallas kernels, body(): pl.pallas_call(kernel, out_shape=jax.ShapeDtypeStruct((512, 512), bf16),...  67.3 us
    unnamed x19, local copies, waits for them, and re-layouts  7.13 us

profile of v3, /device:TPU:1, one launch (start us, length us, event | category | flops | bytes accessed | tf_op | source)
XLA Modules:
  0.0 74.5 jit_solution(14740965403474402310)
XLA Ops:
  0.0 0.0 copy-start.5
  0.0 0.0 copy-start.8
  0.0 0.7 copy-done.5
  0.7 0.0 copy-done.8
  0.7 0.0 copy-start
  0.7 1.0 %copy-done = bf16[512,512]{1,0:T(8,128)(2,1)S(1)} copy-done((bf16[512,512]{1,0:T(8,128)(2,1)S(1)}, bf16[512,512]{1,0:T(8,128)(2,1)}, u32[]{:S(2)}) %copy-start) | copy-done | bytes 524312
  1.7 0.0 copy-start.1
  1.7 0.9 %copy-done.1 = bf16[128,3,256]{2,0,1:T(8,128)(2,1)S(1)} copy-done((bf16[128,3,256]{2,0,1:T(8,128)(2,1)S(1)}, bf16[128,3,256]{2,0,1:T(8,128)(2,1)}, u32[]{:S(2)}) %copy-start.1) | copy-done | bytes 196632
  2.7 0.0 copy-start.2
  2.7 0.8 %copy-done.2 = bf16[256,128]{1,0:T(8,128)(2,1)S(1)} copy-done((bf16[256,128]{1,0:T(8,128)(2,1)S(1)}, bf16[256,128]{1,0:T(8,128)(2,1)}, u32[]{:S(2)}) %copy-start.2) | copy-done | bytes 65560
  3.5 0.0 copy-start.3
  3.5 0.7 copy-done.3
  4.2 0.0 copy-start.4
  4.3 0.7 copy-done.4
  5.0 0.0 copy-start.6
  5.0 0.7 copy-done.6
  5.7 0.0 copy-start.7
  5.7 0.7 copy-done.7
  6.3 67.3 %shard_map.91 = bf16[512,512]{1,0:T(8,128)(2,1)S(1)} custom-call(s32[4,128]{1,0:T(4,128)S(1)} %bitcast.8, f32[32,128]{1,0:T(8,128)S(1)} %bitcast.7, f32[1,256]{1,0:T(1,128)S(1)} %bitcast.9, f32[3,7,256]{2,1,0:T(8,128)S(1)} %bitcast.6, f32[16,16]{1,0:T(8,128)S(1)} %copy-done.5, f32[16,16]{1,0:T(8,128)S(1)} %copy-done.6, bf16[3,128,256]{2,1,0:T(8,128)(2,1)S(1)} %bitcast.5, ...), custom_call_target="tpu_custom_call" | custom-call | tf_op jit(solution)/shard_map/pallas_call | solution.py:509
  73.7 0.8 %copy.11 = bf16[512,512]{1,0:T(8,128)(2,1)} copy(bf16[512,512]{1,0:T(8,128)(2,1)S(1)} %shard_map.91) | data formatting | bytes 1048576
Async XLA Ops:
  0.0 0.7 copy-start.5
  0.0 0.7 copy-start.8
  0.7 1.0 %copy-start = (bf16[512,512]{1,0:T(8,128)(2,1)S(1)}, bf16[512,512]{1,0:T(8,128)(2,1)}, u32[]{:S(2)}) copy-start(bf16[512,512]{1,0:T(8,128)(2,1)} %emb_ref.1) | copy-start | bytes 1572868
  1.7 0.9 %copy-start.1 = (bf16[128,3,256]{2,0,1:T(8,128)(2,1)S(1)}, bf16[128,3,256]{2,0,1:T(8,128)(2,1)}, u32[]{:S(2)}) copy-start(bf16[128,3,256]{2,0,1:T(8,128)(2,1)} %param.12) | copy-start | bytes 589828
  2.7 0.8 %copy-start.2 = (bf16[256,128]{1,0:T(8,128)(2,1)S(1)}, bf16[256,128]{1,0:T(8,128)(2,1)}, u32[]{:S(2)}) copy-start(bf16[256,128]{1,0:T(8,128)(2,1)} %ow_ref.1) | copy-start | bytes 196612
  3.5 0.7 copy-start.3
  4.2 0.7 copy-start.4
  5.0 0.7 copy-start.6
  5.7 0.7 copy-start.7

commit v4 on v3

--- a/solution.py
+++ b/solution.py
@@ -39,6 +39,16 @@
 
 
 def kernel(
+    tokens_in,
+    gain_in,
+    skip_in,
+    taps_in,
+    rates_in,
+    residue_in,
+    w_in,
+    emb_in,
+    ow_ref,
+    out_ref,
     tokens_ref,
     gain_ref,
     skip_ref,
@@ -47,8 +57,6 @@
     residue_ref,
     w_ref,
     emb_ref,
-    ow_ref,
-    out_ref,
     wt,
     wbuf,
     ebuf,
@@ -63,6 +71,7 @@
     table,
     tokens,
     token_mat,
+    token_page,
     one_hot,
     short_in,
     taps,
@@ -75,6 +84,7 @@
     gated,
     wo,
     total,
+    load_sems,
     send_sems,
     recv_sems,
 ):
@@ -122,6 +132,22 @@
     def receive(name, target):
         pltpu.make_async_copy(target, target, recv_sems.at[slot(name)]).wait()
 
+    def load(k, source, target):
+        copy = pltpu.make_async_copy(source, target, load_sems.at[k])
+        copy.start()
+        return copy
+
+    emb_load = load(0, emb_in, emb_ref)
+    w_load = load(1, w_in, w_ref)
+    small_loads = [
+        load(2, tokens_in, tokens_ref),
+        load(3, gain_in, gain_ref),
+        load(4, skip_in, skip_ref),
+        load(5, taps_in, taps_ref),
+        load(6, rates_in, rates_ref),
+        load(7, residue_in, residue_ref),
+    ]
+
     barrier = pltpu.get_barrier_semaphore()
 
     def greet(device):
@@ -138,17 +164,16 @@
     def _():
         greet(swap_to)
 
+    w_load.wait()
     for group in range(3):
         for h in range(2):
             block = w_ref[group, :, h * 128 : (h + 1) * 128].astype(f32)
             wt[group, h * 128 : (h + 1) * 128, :] = block.T.astype(bf16)
-    ones = jnp.ones((8, 512), bf16)
-    piece = emb_ref[...].astype(f32)
-    high, low = split(piece * piece)
-    squares[j] = (dot_nt(ones, high) + dot_nt(ones, low))[0:1, :]
-
+    for copy in small_loads:
+        copy.wait()
     pl.semaphore_wait(barrier, count_ctx - 1 + count_fsdp - 1 + jnp.where(moves, 1, 0))
 
+    emb_load.wait()
     holder = z // share
     e_slots = [slot("e" + str(k)) for k in range(NX)]
     emb_piece = emb_ref.at[:, pl.ds(aligned(z % share, 128), 128)]
@@ -188,9 +213,6 @@
 
     for d in range(1, NZ):
         send("tz" + str(d), tokens_ref, tokens.at[y, z], at(zz=(z + d) % NZ))
-    for d in range(1, count_fsdp):
-        send("sq" + str(d), squares.at[j], squares.at[j], (i, (j + d) % count_fsdp))
-
     wo_rows = pl.ds(aligned(2 * y + z // share, 256), 256)
     wo_cols = pl.ds(aligned(z % share, 128), 128)
     wo_own = wo.at[wo_rows, wo_cols]
@@ -208,6 +230,14 @@
 
     wbuf[y] = wt[:, pl.ds(aligned(y, 64), 64), :]
     tokens[y, z] = tokens_ref[...]
+
+    ones = jnp.ones((8, 512), bf16)
+    piece = emb_ref[...].astype(f32)
+    high, low = split(piece * piece)
+    squares[j] = (dot_nt(ones, high) + dot_nt(ones, low))[0:1, :]
+
+    for d in range(1, count_fsdp):
+        send("sq" + str(d), squares.at[j], squares.at[j], (i, (j + d) % count_fsdp))
 
     row = lax.broadcasted_iota(jnp.int32, (CHUNK, CHUNK), 0)
     lane = lax.broadcasted_iota(jnp.int32, (CHUNK, CHUNK), 1)
@@ -243,6 +273,10 @@
     def _():
         for k in range(NX):
             pltpu.make_async_copy(ebuf.at[k], ebuf.at[k], recv_sems.at[e_slots[k]]).wait()
+
+    receive("swap", wo_own)
+    for d in (2, 6, 1, 7):
+        send("wz" + str(d), wo_own, wo_own, at(zz=(z + d) % NZ))
 
     for k in range(NY):
         gain = gain_ref[pl.ds(k * NZ + z, 1), :]
@@ -276,16 +310,42 @@
     for d in range(1, NY):
         send("ty" + str(d), tokens.at[y], tokens.at[y], at(yy=(y + d) % NY))
 
-    receive("swap", wo_own)
-    for d in (2, 6, 1, 7):
-        send("wz" + str(d), wo_own, wo_own, at(zz=(z + d) % NZ))
+    def wo_place(origin, half=None):
+        rows, first = (256, 0) if half is None else (128, half * 128)
+        return wo.at[
+            pl.ds(aligned(2 * y + origin // share, 256) + first, rows),
+            pl.ds(aligned(origin % share, 128), 128),
+        ]
+
+    for d in (1, 7, 2, 6):
+        receive("wz" + str(d), wo_place((z + NZ - d) % NZ))
+    ahead, behind = at(zz=(z + 2) % NZ), at(zz=(z + NZ - 2) % NZ)
+    block = wo_place((z + NZ - 1) % NZ)
+    send("wz3", block, block, ahead)
+    block = wo_place((z + 1) % NZ)
+    send("wz5", block, block, behind)
+    block = wo_place((z + NZ - 2) % NZ, 0)
+    send("wz4a", block, block, ahead)
+    block = wo_place((z + 2) % NZ, 1)
+    send("wz4b", block, block, behind)
+
+    def along_y(offset):
+        block = wo_place((z + offset) % NZ)
+        send("wy_up%d" % offset, block, block, at(yy=up))
+        send("wy_down%d" % offset, block, block, at(yy=down))
+
+    for offset in (0, 1, 7, 2, 6):
+        along_y(offset)
 
     for d in range(1, NY):
         receive("ty" + str(d), tokens.at[(y + NY - d) % NY])
     for k in range(count_ctx):
-        token_mat[k * 4 : (k + 1) * 4, :] = tokens[k // NZ, k % NZ].astype(f32)
+        these = tokens[k // NZ, k % NZ]
+        token_mat[k * 4 : (k + 1) * 4, :] = (these % 128).astype(f32)
+        token_page[k * 4 : (k + 1) * 4, :] = (these // 128).astype(f32)
     token_mat[...] = token_mat[...].T
-    vocab_row = lax.broadcasted_iota(jnp.int32, (512, 128), 0).astype(f32)
+    token_page[...] = token_page[...].T
+    vocab_row = row.astype(f32)
 
     def mark(n, carry):
         for h in range(2):
@@ -295,13 +355,6 @@
         return carry
 
     lax.fori_loop(0, 64, mark, 0)
-
-    def wo_place(origin, half=None):
-        rows, first = (256, 0) if half is None else (128, half * 128)
-        return wo.at[
-            pl.ds(aligned(2 * y + origin // share, 256) + first, rows),
-            pl.ds(aligned(origin % share, 128), 128),
-        ]
 
     for d in range(1, count_fsdp):
         receive("sq" + str(d), squares.at[(j + count_fsdp - d) % count_fsdp])
@@ -323,28 +376,28 @@
         receive("q" + str(d), arrived_q.at[origin])
         value = value + arrived_q[origin].astype(f32)
     table[0:8, :] = jnp.concatenate([value[0:8], value[8:16]], axis=1) * scale
-    table[24:32, :] = jnp.zeros((8, 512), f32)
-
-    for d in (1, 7, 2, 6):
-        receive("wz" + str(d), wo_place((z + NZ - d) % NZ))
-    ahead, behind = at(zz=(z + 2) % NZ), at(zz=(z + NZ - 2) % NZ)
-    block = wo_place((z + NZ - 1) % NZ)
-    send("wz3", block, block, ahead)
-    block = wo_place((z + 1) % NZ)
-    send("wz5", block, block, behind)
-    block = wo_place((z + NZ - 2) % NZ, 0)
-    send("wz4a", block, block, ahead)
-    block = wo_place((z + 2) % NZ, 1)
-    send("wz4b", block, block, behind)
-
-    table16 = table[...].astype(bf16)
+
+    receive("wz3", wo_place((z + NZ - 3) % NZ))
+    receive("wz5", wo_place((z + 3) % NZ))
+    receive("wz4a", wo_place((z + 4) % NZ, 0))
+    receive("wz4b", wo_place((z + 4) % NZ, 1))
+    for offset in (3, 5, 4):
+        along_y(offset)
+
+    pages = [table[0:24, k * 128 : (k + 1) * 128] for k in range(4)]
+    table16 = jnp.concatenate(pages, axis=0).astype(bf16)
 
     def look_up(n, carry):
         found = dot(table16, one_hot[n])
-        for group in range(3):
-            for h in range(2):
-                rows = pl.ds(aligned(2 * n + h + 8, 8), 8)
-                short_in[group, rows, :] = found[group * 8 : (group + 1) * 8, h * 128 : (h + 1) * 128]
+        for h in range(2):
+            page = jnp.broadcast_to(token_page[pl.ds(2 * n + h, 1), :], (24, 128))
+            options = [found[k * 24 : (k + 1) * 24, h * 128 : (h + 1) * 128] for k in range(4)]
+            low = jnp.where(page == 0.0, options[0], options[1])
+            high = jnp.where(page == 2.0, options[2], options[3])
+            value = jnp.where(page < 2.0, low, high)
+            rows = pl.ds(aligned(2 * n + h + 8, 8), 8)
+            for group in range(3):
+                short_in[group, rows, :] = value[group * 8 : (group + 1) * 8]
         return carry
 
     lax.fori_loop(0, 64, look_up, 0, unroll=4)
@@ -369,14 +422,6 @@
 
     lax.fori_loop(0, 128, convolve, 0, unroll=4)
 
-    receive("wz3", wo_place((z + NZ - 3) % NZ))
-    receive("wz5", wo_place((z + 3) % NZ))
-    receive("wz4a", wo_place((z + 4) % NZ, 0))
-    receive("wz4b", wo_place((z + 4) % NZ, 1))
-    wo_line = wo.at[pl.ds(aligned(y, 512), 512), :]
-    send("wy_up", wo_line, wo_line, at(yy=up))
-    send("wy_down", wo_line, wo_line, at(yy=down))
-
     planes = [driving[pl.ds(k, CHUNK, stride=8), :] for k in range(8)]
     wide = jnp.concatenate(planes, axis=1)
     ends = dot_three(to_end, wide)
@@ -423,12 +468,21 @@
     send("g_left0", own[0], own[0], at(xx=left))
     send("g_mate", gated.at[j], gated.at[j], at(cc=1 - c))
 
-    wo_down = pl.ds(aligned(down, 512), 512)
-    wo_up = pl.ds(aligned(up, 512), 512)
-    receive("wy_up", wo.at[wo_down, :])
+    def from_y(name, line):
+        for offset in range(NZ):
+            origin = (z + offset) % NZ
+            receive(
+                name + str(offset),
+                wo.at[
+                    pl.ds(aligned(2 * line + origin // share, 256), 256),
+                    pl.ds(aligned(origin % share, 128), 128),
+                ],
+            )
+
+    from_y("wy_up", down)
     block = wo.at[pl.ds(aligned(2 * down, 256), 256), :]
     send("wy_on_up", block, block, at(yy=up))
-    receive("wy_down", wo.at[wo_up, :])
+    from_y("wy_down", up)
     block = wo.at[pl.ds(aligned(2 * up + 1, 256), 256), :]
     send("wy_on_down", block, block, at(yy=down))
 
@@ -489,7 +543,7 @@
         swap_copy().wait_send()
 
 
-SEMAPHORES = 160
+SEMAPHORES = 180
 
 
 def body(
@@ -509,9 +563,17 @@
     return pl.pallas_call(
         kernel,
         out_shape=jax.ShapeDtypeStruct((512, 512), bf16),
-        in_specs=[whole] * 8 + [outside],
+        in_specs=[outside] * 9,
         out_specs=whole,
         scratch_shapes=[
+            vm((4, 128), jnp.int32),
+            vm((32, 128), f32),
+            vm((1, 256), f32),
+            vm((3, 7, 256), f32),
+            vm((16, 16), f32),
+            vm((16, 16), f32),
+            vm((3, 128, 256), bf16),
+            vm((512, 512), bf16),
             vm((3, 256, 128), bf16),
             vm((NY, 3, 64, 128), bf16),
             vm((NX, 512, 128), bf16),
@@ -523,10 +585,11 @@
             vm((NZ, 16, 256), bf16),
             vm((16, 512), f32),
             vm((16, 256), f32),
-            vm((32, 512), f32),
+            vm((24, 512), f32),
             vm((NY, NZ, 4, 128), jnp.int32),
             vm((128, 128), f32),
-            vm((64, 512, 256), bf16),
+            vm((128, 128), f32),
+            vm((64, 128, 256), bf16),
             vm((3, 1088, 128), f32),
             vm((3, 7, 8, 128), f32),
             vm((1024, 128), f32),
@@ -538,11 +601,12 @@
             vm((NX * NC, 512, 256), bf16),
             vm((2048, 512), bf16),
             vm((512, 512), f32),
+            pltpu.SemaphoreType.DMA((8,)),
             pltpu.SemaphoreType.DMA((SEMAPHORES,)),
             pltpu.SemaphoreType.DMA((SEMAPHORES,)),
         ],
         compiler_params=pltpu.CompilerParams(
-            collective_id=0, has_side_effects=True, vmem_limit_bytes=48 * 1024 * 1024
+            collective_id=0, has_side_effects=True, vmem_limit_bytes=60 * 1024 * 1024
         ),
     )(
         tokens.reshape(4, 128),

time: 74.9 us -> 67 us (0.89)
  local copies, waits for them, and re-layouts: 7.13 us -> 1.87 us
  Pallas kernels: 67.3 us -> 65 us
    unnamed x19 -> x1, local copies, waits for them, and re-layouts: 7.13 us -> 1.87 us
    pallas_call x1, Pallas kernels: 67.3 us -> 65 us  [body(): pl.pallas_call(kernel, out_shape=jax.ShapeDtypeStruct((512, 512), bf16),...]
where the time goes in v4:
time: 67 us; the launch traced here: 66.8 us
  Pallas kernels  65 us (97%)
  local copies, waits for them, and re-layouts  1.87 us (3%)
    pallas_call x1, Pallas kernels, body(): pl.pallas_call(kernel, out_shape=jax.ShapeDtypeStruct((512, 512), bf16),...  65 us
    unnamed x1, local copies, waits for them, and re-layouts  1.87 us

profile of v4, /device:TPU:1, one launch (start us, length us, event | category | flops | bytes accessed | tf_op | source)
XLA Modules:
  0.0 66.8 jit_solution(8556699362693000392)
XLA Ops:
  0.0 65.0 %shard_map.91 = bf16[512,512]{1,0:T(8,128)(2,1)} custom-call(s32[4,128]{1,0:T(4,128)} %bitcast.8, f32[32,128]{1,0:T(8,128)} %bitcast.7, f32[1,256]{1,0:T(1,128)} %bitcast.9, f32[3,7,256]{2,1,0:T(8,128)} %bitcast.6, f32[16,16]{1,0:T(8,128)} %rates_in.1, f32[16,16]{1,0:T(8,128)} %residue_in.1, bf16[3,128,256]{2,1,0:T(8,128)(2,1)} %bitcast.5, ...), custom_call_target="tpu_custom_call" | custom-call | tf_op jit(solution)/shard_map/pallas_call | solution.py:563
  65.0 1.9 %copy.11 = bf16[512,512]{1,0:T(8,128)(2,1)} copy(bf16[512,512]{1,0:T(8,128)(2,1)} %shard_map.91) | data formatting | bytes 1048576

commit v5 on v4

--- a/solution.py
+++ b/solution.py
@@ -173,6 +173,21 @@
         copy.wait()
     pl.semaphore_wait(barrier, count_ctx - 1 + count_fsdp - 1 + jnp.where(moves, 1, 0))
 
+    wo_rows = pl.ds(aligned(2 * y + z // share, 256), 256)
+    wo_cols = pl.ds(aligned(z % share, 128), 128)
+    wo_own = wo.at[wo_rows, wo_cols]
+
+    def swap_copy():
+        return remote("swap", ow_ref, wo.at[pl.ds(aligned(j, 256), 256), wo_cols], swap_to)
+
+    @pl.when(moves)
+    def _():
+        swap_copy().start()
+
+    @pl.when(jnp.logical_not(moves))
+    def _():
+        pltpu.make_async_copy(ow_ref, wo_own, recv_sems.at[slot("swap")]).start()
+
     emb_load.wait()
     holder = z // share
     e_slots = [slot("e" + str(k)) for k in range(NX)]
@@ -213,21 +228,6 @@
 
     for d in range(1, NZ):
         send("tz" + str(d), tokens_ref, tokens.at[y, z], at(zz=(z + d) % NZ))
-    wo_rows = pl.ds(aligned(2 * y + z // share, 256), 256)
-    wo_cols = pl.ds(aligned(z % share, 128), 128)
-    wo_own = wo.at[wo_rows, wo_cols]
-
-    def swap_copy():
-        return remote("swap", ow_ref, wo.at[pl.ds(aligned(j, 256), 256), wo_cols], swap_to)
-
-    @pl.when(moves)
-    def _():
-        swap_copy().start()
-
-    @pl.when(jnp.logical_not(moves))
-    def _():
-        pltpu.make_async_copy(ow_ref, wo_own, recv_sems.at[slot("swap")]).start()
-
     wbuf[y] = wt[:, pl.ds(aligned(y, 64), 64), :]
     tokens[y, z] = tokens_ref[...]
 
@@ -262,6 +262,10 @@
             value = jnp.where(pick, taps_ref[group, lag : lag + 1, :], 0.0)
             taps[group, lag] = jnp.broadcast_to(jnp.sum(value, axis=1, keepdims=True), (8, CHUNK))
 
+    receive("swap", wo_own)
+    for d in (2, 6, 1, 7):
+        send("wz" + str(d), wo_own, wo_own, at(zz=(z + d) % NZ))
+
     @pl.when(c == holder)
     def _():
         pltpu.make_async_copy(ebuf.at[x], ebuf.at[x], recv_sems.at[e_slots[0] + x]).wait()
@@ -273,10 +277,6 @@
     def _():
         for k in range(NX):
             pltpu.make_async_copy(ebuf.at[k], ebuf.at[k], recv_sems.at[e_slots[k]]).wait()
-
-    receive("swap", wo_own)
-    for d in (2, 6, 1, 7):
-        send("wz" + str(d), wo_own, wo_own, at(zz=(z + d) % NZ))
 
     for k in range(NY):
         gain = gain_ref[pl.ds(k * NZ + z, 1), :]
@@ -310,33 +310,6 @@
     for d in range(1, NY):
         send("ty" + str(d), tokens.at[y], tokens.at[y], at(yy=(y + d) % NY))
 
-    def wo_place(origin, half=None):
-        rows, first = (256, 0) if half is None else (128, half * 128)
-        return wo.at[
-            pl.ds(aligned(2 * y + origin // share, 256) + first, rows),
-            pl.ds(aligned(origin % share, 128), 128),
-        ]
-
-    for d in (1, 7, 2, 6):
-        receive("wz" + str(d), wo_place((z + NZ - d) % NZ))
-    ahead, behind = at(zz=(z + 2) % NZ), at(zz=(z + NZ - 2) % NZ)
-    block = wo_place((z + NZ - 1) % NZ)
-    send("wz3", block, block, ahead)
-    block = wo_place((z + 1) % NZ)
-    send("wz5", block, block, behind)
-    block = wo_place((z + NZ - 2) % NZ, 0)
-    send("wz4a", block, block, ahead)
-    block = wo_place((z + 2) % NZ, 1)
-    send("wz4b", block, block, behind)
-
-    def along_y(offset):
-        block = wo_place((z + offset) % NZ)
-        send("wy_up%d" % offset, block, block, at(yy=up))
-        send("wy_down%d" % offset, block, block, at(yy=down))
-
-    for offset in (0, 1, 7, 2, 6):
-        along_y(offset)
-
     for d in range(1, NY):
         receive("ty" + str(d), tokens.at[(y + NY - d) % NY])
     for k in range(count_ctx):
@@ -345,6 +318,23 @@
         token_page[k * 4 : (k + 1) * 4, :] = (these // 128).astype(f32)
     token_mat[...] = token_mat[...].T
     token_page[...] = token_page[...].T
+    def wo_place(origin, half=None):
+        rows, first = (256, 0) if half is None else (128, half * 128)
+        return wo.at[
+            pl.ds(aligned(2 * y + origin // share, 256) + first, rows),
+            pl.ds(aligned(origin % share, 128), 128),
+        ]
+
+    for d in (1, 7, 2, 6):
+        receive("wz" + str(d), wo_place((z + NZ - d) % NZ))
+    def along_y(offset):
+        block = wo_place((z + offset) % NZ)
+        send("wy_up%d" % offset, block, block, at(yy=up))
+        send("wy_down%d" % offset, block, block, at(yy=down))
+
+    for offset in (0, 1, 7, 2, 6):
+        along_y(offset)
+
     vocab_row = row.astype(f32)
 
     def mark(n, carry):
@@ -377,12 +367,15 @@
         value = value + arrived_q[origin].astype(f32)
     table[0:8, :] = jnp.concatenate([value[0:8], value[8:16]], axis=1) * scale
 
-    receive("wz3", wo_place((z + NZ - 3) % NZ))
-    receive("wz5", wo_place((z + 3) % NZ))
-    receive("wz4a", wo_place((z + 4) % NZ, 0))
-    receive("wz4b", wo_place((z + 4) % NZ, 1))
-    for offset in (3, 5, 4):
-        along_y(offset)
+    ahead, behind = at(zz=(z + 2) % NZ), at(zz=(z + NZ - 2) % NZ)
+    block = wo_place((z + NZ - 1) % NZ)
+    send("wz3", block, block, ahead)
+    block = wo_place((z + 1) % NZ)
+    send("wz5", block, block, behind)
+    block = wo_place((z + NZ - 2) % NZ, 0)
+    send("wz4a", block, block, ahead)
+    block = wo_place((z + 2) % NZ, 1)
+    send("wz4b", block, block, behind)
 
     pages = [table[0:24, k * 128 : (k + 1) * 128] for k in range(4)]
     table16 = jnp.concatenate(pages, axis=0).astype(bf16)
@@ -444,29 +437,60 @@
         gated_f[pl.ds(k, CHUNK, stride=8), :] = result.T
     gated_b[...] = gated_f[...].astype(bf16)
 
-    def positions(index):
-        return gated_b.at[pl.ds(aligned(index, 32), 32), :]
-
     far = sorted(range(1, count_ctx), key=lambda d: -min(d % NZ, NZ - d % NZ))
-    for d in far:
-        to = (i + d) % count_ctx
-        send("a" + str(d), positions(to), landed.at[i], (to, j))
+    for part in range(2):
+        for d in far:
+            to = (i + d) % count_ctx
+            rows = pl.ds(aligned(2 * to + part, 16), 16)
+            send("a%d_%d" % (part, d), gated_b.at[rows, :], landed.at[i, pl.ds(16 * part, 16), :], (to, j))
+    receive("wz3", wo_place((z + NZ - 3) % NZ))
+    receive("wz5", wo_place((z + 3) % NZ))
+    receive("wz4a", wo_place((z + 4) % NZ, 0))
+    receive("wz4b", wo_place((z + 4) % NZ, 1))
+    for offset in (3, 5, 4):
+        along_y(offset)
+
     landed[i] = gated_b[pl.ds(aligned(i, 32), 32), :]
-    for d in reversed(far):
-        receive("a" + str(d), landed.at[(i + count_ctx - d) % count_ctx])
-    for k in range(4):
-        for h in range(2):
-            blocks = [landed[n].astype(f32)[k * 8 : (k + 1) * 8] for n in range(h * 16, (h + 1) * 16)]
-            block = jnp.concatenate(blocks, axis=0)
-            gated[j, k * 128 : (k + 1) * 128, h * 128 : (h + 1) * 128] = block.T.astype(bf16)
-
-    halves = (pl.ds(0, 256), pl.ds(256, 256))
-    own = [gated.at[j, half, :] for half in halves]
-    send("g_right0", own[0], own[0], at(xx=right))
-    send("g_left1", own[1], own[1], at(xx=left))
-    send("g_right1", own[1], own[1], at(xx=right))
-    send("g_left0", own[0], own[0], at(xx=left))
-    send("g_mate", gated.at[j], gated.at[j], at(cc=1 - c))
+
+    left_j, right_j, across_j = left * NC + c, right * NC + c, across * NC + c
+    mate_j = x * NC + 1 - c
+    to_right, to_left = at(xx=right), at(xx=left)
+
+    def quarter(index, k):
+        return gated.at[index, pl.ds(128 * k, 128), :]
+
+    def half(index, part):
+        return gated.at[index, pl.ds(256 * part, 256), :]
+
+    early = len(sent)
+    for part in range(2):
+        for d in reversed(far):
+            origin = (i + count_ctx - d) % count_ctx
+            receive("a%d_%d" % (part, d), landed.at[origin, pl.ds(16 * part, 16), :])
+        blocks = [landed[n, part * 16 : part * 16 + 16, :].astype(f32) for n in range(count_ctx)]
+        for k in range(2):
+            for h in range(2):
+                block = [blocks[n][k * 8 : (k + 1) * 8] for n in range(h * 16, (h + 1) * 16)]
+                block = jnp.concatenate(block, axis=0)
+                rows = slice((2 * part + k) * 128, (2 * part + k + 1) * 128)
+                gated[j, rows, h * 128 : (h + 1) * 128] = block.T.astype(bf16)
+        first, second = 2 * part, 2 * part + 1
+        send("g_right%d" % first, quarter(j, first), quarter(j, first), to_right)
+        send("g_left%d" % second, quarter(j, second), quarter(j, second), to_left)
+        send("g_right%d" % second, quarter(j, second), quarter(j, second), to_right)
+        send("g_left%d" % first, quarter(j, first), quarter(j, first), to_left)
+        send("g_mate%d" % part, half(j, part), half(j, part), mate)
+
+    def relay_x(part):
+        first, second = 2 * part, 2 * part + 1
+        receive("g_right%d" % first, quarter(left_j, first))
+        send("g_on_right%d" % part, quarter(left_j, first), quarter(left_j, first), to_right)
+        receive("g_left%d" % second, quarter(right_j, second))
+        send("g_on_left%d" % part, quarter(right_j, second), quarter(right_j, second), to_left)
+        receive("g_right%d" % second, quarter(left_j, second))
+        send("m_left%d" % part, half(left_j, part), half(left_j, part), mate)
+        receive("g_left%d" % first, quarter(right_j, first))
+        send("m_right%d" % part, half(right_j, part), half(right_j, part), mate)
 
     def from_y(name, line):
         for offset in range(NZ):
@@ -486,64 +510,56 @@
     block = wo.at[pl.ds(aligned(2 * up + 1, 256), 256), :]
     send("wy_on_down", block, block, at(yy=down))
 
-    left_j, right_j, across_j = left * NC + c, right * NC + c, across * NC + c
-    from_left = [gated.at[left_j, half, :] for half in halves]
-    from_right = [gated.at[right_j, half, :] for half in halves]
-    from_across = [gated.at[across_j, half, :] for half in halves]
-    receive("g_right0", from_left[0])
-    send("g_on_right", from_left[0], from_left[0], at(xx=right))
-    receive("g_left1", from_right[1])
-    send("g_on_left", from_right[1], from_right[1], at(xx=left))
-    send("m_left0", from_left[0], from_left[0], mate)
-    send("m_right1", from_right[1], from_right[1], mate)
-    receive("g_right1", from_left[1])
-    send("m_left1", from_left[1], from_left[1], mate)
-    receive("g_left0", from_right[0])
-    send("m_right0", from_right[0], from_right[0], mate)
+    relay_x(0)
+
+    relay_x(1)
+
+    def product(index):
+        return dot(gated[index], wo[pl.ds(aligned(index, 256), 256), :])
+
+    for copy in sent[:early]:
+        copy.wait_send()
+
+    @pl.when(c == holder)
+    def _():
+        for copy in emb_copies():
+            copy.wait_send()
+        for _, copy in emb_relays():
+            copy.wait_send()
+
+    @pl.when(moves)
+    def _():
+        swap_copy().wait_send()
 
     receive("wy_on_up", wo.at[pl.ds(aligned(2 * opposite, 256), 256), :])
     receive("wy_on_down", wo.at[pl.ds(aligned(2 * opposite + 1, 256), 256), :])
-
-    def product(index):
-        return dot(gated[index], wo[pl.ds(aligned(index, 256), 256), :])
-
-    mate_j = x * NC + 1 - c
     total[...] = product(j)
-    receive("g_mate", gated.at[mate_j])
+    total[...] += product(left_j)
+    for part in range(2):
+        receive("g_on_right%d" % part, quarter(across_j, 2 * part))
+        receive("g_on_left%d" % part, quarter(across_j, 2 * part + 1))
+        send("m_across%d" % part, half(across_j, part), half(across_j, part), mate)
+        if part == 0:
+            total[...] += product(right_j)
+    receive("g_mate0", half(mate_j, 0))
+    receive("g_mate1", half(mate_j, 1))
     total[...] += product(mate_j)
-    total[...] += product(left_j)
-    total[...] += product(right_j)
-    receive("g_on_right", from_across[0])
-    send("m_across0", from_across[0], from_across[0], mate)
-    receive("g_on_left", from_across[1])
-    send("m_across1", from_across[1], from_across[1], mate)
     for name, place in (("left", left), ("right", right), ("across", across)):
         index = place * NC + 1 - c
         if name == "across":
             total[...] += product(across_j)
-        receive("m_" + name + "0", gated.at[index, halves[0], :])
-        receive("m_" + name + "1", gated.at[index, halves[1], :])
+        receive("m_" + name + "0", half(index, 0))
+        receive("m_" + name + "1", half(index, 1))
         if name == "across":
             out_ref[...] = (total[...] + product(index)).astype(bf16)
         else:
             total[...] += product(index)
 
-    for copy in sent:
+    for copy in sent[early:]:
         copy.wait_send()
 
-    @pl.when(c == holder)
-    def _():
-        for copy in emb_copies():
-            copy.wait_send()
-        for _, copy in emb_relays():
-            copy.wait_send()
-
-    @pl.when(moves)
-    def _():
-        swap_copy().wait_send()
-
-
-SEMAPHORES = 180
+
+SEMAPHORES = 240
 
 
 def body(

time: 67 us -> 62.1 us (0.927)
  Pallas kernels: 65 us -> 60 us
    pallas_call x1, Pallas kernels: 65 us -> 60 us  [body(): pl.pallas_call(kernel, out_shape=jax.ShapeDtypeStruct((512, 512), bf16),...]
where the time goes in v5:
time: 62.1 us; the launch traced here: 61.9 us
  Pallas kernels  60 us (97%)
  local copies, waits for them, and re-layouts  1.87 us (3%)
    pallas_call x1, Pallas kernels, body(): pl.pallas_call(kernel, out_shape=jax.ShapeDtypeStruct((512, 512), bf16),...  60 us
    unnamed x1, local copies, waits for them, and re-layouts  1.87 us

profile of v5, /device:TPU:1, one launch (start us, length us, event | category | flops | bytes accessed | tf_op | source)
XLA Modules:
  0.0 61.9 jit_solution(5203600535888494683)
XLA Ops:
  0.0 60.0 %shard_map.91 = bf16[512,512]{1,0:T(8,128)(2,1)} custom-call(s32[4,128]{1,0:T(4,128)} %bitcast.8, f32[32,128]{1,0:T(8,128)} %bitcast.7, f32[1,256]{1,0:T(1,128)} %bitcast.9, f32[3,7,256]{2,1,0:T(8,128)} %bitcast.6, f32[16,16]{1,0:T(8,128)} %rates_in.1, f32[16,16]{1,0:T(8,128)} %residue_in.1, bf16[3,128,256]{2,1,0:T(8,128)(2,1)} %bitcast.5, ...), custom_call_target="tpu_custom_call" | custom-call | tf_op jit(solution)/shard_map/pallas_call | solution.py:579
  60.0 1.9 %copy.11 = bf16[512,512]{1,0:T(8,128)(2,1)} copy(bf16[512,512]{1,0:T(8,128)(2,1)} %shard_map.91) | data formatting | bytes 1048576

commit v6 on v5

--- a/solution.py
+++ b/solution.py
@@ -153,8 +153,10 @@
     def greet(device):
         pl.semaphore_signal(barrier, inc=1, device_id=device, device_id_type=MESH)
 
-    for d in range(1, count_ctx):
-        greet(((i + d) % count_ctx, j))
+    for d in range(1, NZ):
+        greet(at(zz=(z + d) % NZ))
+    for d in range(1, NY):
+        greet(at(yy=(y + d) % NY))
     for d in range(1, count_fsdp):
         greet((i, (j + d) % count_fsdp))
     swap_to = (share * j + i % share, i // share)
@@ -171,7 +173,7 @@
             wt[group, h * 128 : (h + 1) * 128, :] = block.T.astype(bf16)
     for copy in small_loads:
         copy.wait()
-    pl.semaphore_wait(barrier, count_ctx - 1 + count_fsdp - 1 + jnp.where(moves, 1, 0))
+    pl.semaphore_wait(barrier, NZ - 1 + NY - 1 + count_fsdp - 1 + jnp.where(moves, 1, 0))
 
     wo_rows = pl.ds(aligned(2 * y + z // share, 256), 256)
     wo_cols = pl.ds(aligned(z % share, 128), 128)

time: 62.1 us -> 59.9 us (0.965)
  Pallas kernels: 60 us -> 57.8 us
    pallas_call x1, Pallas kernels: 60 us -> 57.8 us  [body(): pl.pallas_call(kernel, out_shape=jax.ShapeDtypeStruct((512, 512), bf16),...]
where the time goes in v6:
time: 59.9 us; the launch traced here: 59.7 us
  Pallas kernels  57.8 us (96%)
  local copies, waits for them, and re-layouts  1.87 us (3%)
    pallas_call x1, Pallas kernels, body(): pl.pallas_call(kernel, out_shape=jax.ShapeDtypeStruct((512, 512), bf16),...  57.8 us
    unnamed x1, local copies, waits for them, and re-layouts  1.87 us

profile of v6, /device:TPU:1, one launch (start us, length us, event | category | flops | bytes accessed | tf_op | source)
XLA Modules:
  0.0 59.7 jit_solution(8191921308139409996)
XLA Ops:
  0.0 57.8 %shard_map.91 = bf16[512,512]{1,0:T(8,128)(2,1)} custom-call(s32[4,128]{1,0:T(4,128)} %bitcast.8, f32[32,128]{1,0:T(8,128)} %bitcast.7, f32[1,256]{1,0:T(1,128)} %bitcast.9, f32[3,7,256]{2,1,0:T(8,128)} %bitcast.6, f32[16,16]{1,0:T(8,128)} %rates_in.1, f32[16,16]{1,0:T(8,128)} %residue_in.1, bf16[3,128,256]{2,1,0:T(8,128)(2,1)} %bitcast.5, ...), custom_call_target="tpu_custom_call" | custom-call | tf_op jit(solution)/shard_map/pallas_call | solution.py:581
  57.8 1.9 %copy.11 = bf16[512,512]{1,0:T(8,128)(2,1)} copy(bf16[512,512]{1,0:T(8,128)(2,1)} %shard_map.91) | data formatting | bytes 1048576

commit v7 on v6

--- a/solution.py
+++ b/solution.py
@@ -346,7 +346,7 @@
             one_hot[n, :, h * 128 : (h + 1) * 128] = hits.astype(bf16)
         return carry
 
-    lax.fori_loop(0, 64, mark, 0)
+    lax.fori_loop(0, 64, mark, 0, unroll=2)
 
     for d in range(1, count_fsdp):
         receive("sq" + str(d), squares.at[(j + count_fsdp - d) % count_fsdp])
@@ -395,7 +395,7 @@
                 short_in[group, rows, :] = value[group * 8 : (group + 1) * 8]
         return carry
 
-    lax.fori_loop(0, 64, look_up, 0, unroll=4)
+    lax.fori_loop(0, 64, look_up, 0, unroll=16)
     for group in range(3):
         tail = short_in[group, 1024:1088, :]
         shifted = pltpu.roll(tail, 1, 1)
@@ -415,7 +415,7 @@
         driving[here, :] = sums[1] * sums[2]
         return carry
 
-    lax.fori_loop(0, 128, convolve, 0, unroll=4)
+    lax.fori_loop(0, 128, convolve, 0, unroll=16)
 
     planes = [driving[pl.ds(k, CHUNK, stride=8), :] for k in range(8)]
     wide = jnp.concatenate(planes, axis=1)

time: 59.9 us -> 58.3 us (0.973)
  Pallas kernels: 57.8 us -> 56.3 us
    pallas_call x1, Pallas kernels: 57.8 us -> 56.3 us  [body(): pl.pallas_call(kernel, out_shape=jax.ShapeDtypeStruct((512, 512), bf16),...]
where the time goes in v7:
time: 58.3 us; the launch traced here: 58.1 us
  Pallas kernels  56.3 us (97%)
  local copies, waits for them, and re-layouts  1.87 us (3%)
    pallas_call x1, Pallas kernels, body(): pl.pallas_call(kernel, out_shape=jax.ShapeDtypeStruct((512, 512), bf16),...  56.3 us
    unnamed x1, local copies, waits for them, and re-layouts  1.87 us

profile of v7, /device:TPU:1, one launch (start us, length us, event | category | flops | bytes accessed | tf_op | source)
XLA Modules:
  0.0 58.1 jit_solution(13164000810803019352)
XLA Ops:
  0.0 56.3 %shard_map.91 = bf16[512,512]{1,0:T(8,128)(2,1)} custom-call(s32[4,128]{1,0:T(4,128)} %bitcast.8, f32[32,128]{1,0:T(8,128)} %bitcast.7, f32[1,256]{1,0:T(1,128)} %bitcast.9, f32[3,7,256]{2,1,0:T(8,128)} %bitcast.6, f32[16,16]{1,0:T(8,128)} %rates_in.1, f32[16,16]{1,0:T(8,128)} %residue_in.1, bf16[3,128,256]{2,1,0:T(8,128)(2,1)} %bitcast.5, ...), custom_call_target="tpu_custom_call" | custom-call | tf_op jit(solution)/shard_map/pallas_call | solution.py:581
  56.3 1.9 %copy.11 = bf16[512,512]{1,0:T(8,128)(2,1)} copy(bf16[512,512]{1,0:T(8,128)(2,1)} %shard_map.91) | data formatting | bytes 1048576

commit v8 on v7

--- a/solution.py
+++ b/solution.py
@@ -346,7 +346,7 @@
             one_hot[n, :, h * 128 : (h + 1) * 128] = hits.astype(bf16)
         return carry
 
-    lax.fori_loop(0, 64, mark, 0, unroll=2)
+    lax.fori_loop(0, 64, mark, 0, unroll=4)
 
     for d in range(1, count_fsdp):
         receive("sq" + str(d), squares.at[(j + count_fsdp - d) % count_fsdp])
@@ -395,7 +395,7 @@
                 short_in[group, rows, :] = value[group * 8 : (group + 1) * 8]
         return carry
 
-    lax.fori_loop(0, 64, look_up, 0, unroll=16)
+    lax.fori_loop(0, 64, look_up, 0, unroll=32)
     for group in range(3):
         tail = short_in[group, 1024:1088, :]
         shifted = pltpu.roll(tail, 1, 1)
@@ -415,7 +415,7 @@
         driving[here, :] = sums[1] * sums[2]
         return carry
 
-    lax.fori_loop(0, 128, convolve, 0, unroll=16)
+    lax.fori_loop(0, 128, convolve, 0, unroll=32)
 
     planes = [driving[pl.ds(k, CHUNK, stride=8), :] for k in range(8)]
     wide = jnp.concatenate(planes, axis=1)

time: 58.3 us -> 58.3 us (level)
  no operation moved by 1% of the time
where the time goes in v8:
time: 58.3 us; the launch traced here: 58.1 us
  Pallas kernels  56.3 us (97%)
  local copies, waits for them, and re-layouts  1.87 us (3%)
    pallas_call x1, Pallas kernels, body(): pl.pallas_call(kernel, out_shape=jax.ShapeDtypeStruct((512, 512), bf16),...  56.3 us
    unnamed x1, local copies, waits for them, and re-layouts  1.87 us

profile of v8, /device:TPU:1, one launch (start us, length us, event | category | flops | bytes accessed | tf_op | source)
XLA Modules:
  0.0 58.1 jit_solution(12114263185012899807)
XLA Ops:
  0.0 56.3 %shard_map.91 = bf16[512,512]{1,0:T(8,128)(2,1)} custom-call(s32[4,128]{1,0:T(4,128)} %bitcast.8, f32[32,128]{1,0:T(8,128)} %bitcast.7, f32[1,256]{1,0:T(1,128)} %bitcast.9, f32[3,7,256]{2,1,0:T(8,128)} %bitcast.6, f32[16,16]{1,0:T(8,128)} %rates_in.1, f32[16,16]{1,0:T(8,128)} %residue_in.1, bf16[3,128,256]{2,1,0:T(8,128)(2,1)} %bitcast.5, ...), custom_call_target="tpu_custom_call" | custom-call | tf_op jit(solution)/shard_map/pallas_call | solution.py:581
  56.3 1.9 %copy.11 = bf16[512,512]{1,0:T(8,128)(2,1)} copy(bf16[512,512]{1,0:T(8,128)(2,1)} %shard_map.91) | data formatting | bytes 1048576
